TPU v7x, 256 devices: a whole 4x4x8 slice. The times are simulated.
256 devices in a mesh: hid: 16 (over x, y), ffn: 16 (over z, core).
Axes of the slice: x: 4, y: 4, z: 8, core: 2. Of those that a mesh axis runs over, the one named last changes fastest.
Arguments:
- activations: bfloat16 [1024, 10240], P('ffn', 'hid'), may hold values from -12 to 12
- ln_gain: float32 [10240], P('hid'), may hold values from 0.1 to 1.9
- segments: int32 [1024], replicated, may hold values from 0 to 3, never falling along the last dimension, each value on 1 to 512 neighbouring positions
- w_query: bfloat16 [10240, 12288], P('hid', 'ffn'), may hold values from -0.0625 to 0.0625
- w_key_value: bfloat16 [10240, 512], P('hid'), may hold values from -0.0625 to 0.0625
- w_gate: bfloat16 [10240, 36864], P('hid', 'ffn'), may hold values from -0.0625 to 0.0625
- w_up: bfloat16 [10240, 36864], P('hid', 'ffn'), may hold values from -0.0625 to 0.0625
- w_out: bfloat16 [12288, 10240], P('ffn', 'hid'), may hold values from -0.0546875 to 0.0546875
- w_down: bfloat16 [36864, 10240], P('ffn', 'hid'), may hold values from -0.03125 to 0.03125
Outputs:
- block_out: bfloat16 [1024, 10240], P('ffn', 'hid')
Inputs may be any that keep to these rules, and one draw needn't show every extreme that they name: `segments`: document numbers never fall along the tokens; each document has 1 to 512 tokens, one exactly 512.
All inputs are finite; a program needn't handle non-finite values.
Results may differ from a plain program's by a relative error of at most 0.015.
Values may be sent and summed in bfloat16 or wider, within the bound.
A program may use at most 128 MiB of HBM per device.

v0:
```python
import jax
import jax.numpy as jnp
from jax import lax
from jax.sharding import PartitionSpec as P

D = 10240


EPSILON = 1e-06


def rotate(vector, positions):
    half_width = vector.shape[-1] // 2
    frequency = 10000.0 ** (-jnp.arange(half_width, dtype=jnp.float32) / half_width)
    angles = positions[..., None] * frequency
    cosine = jnp.cos(angles)
    sine = jnp.sin(angles)
    first_half = vector[..., :half_width]
    second_half = vector[..., half_width:]
    return jnp.concatenate(
        [first_half * cosine - second_half * sine, first_half * sine + second_half * cosine], -1
    )


def finish_pairs(key_value, positions):
    head_width = key_value.shape[1] // 2
    turned = rotate(key_value[:, :head_width], positions)
    return jnp.concatenate([turned, key_value[:, head_width:]], 1).astype(jnp.bfloat16)


def row_products(gathered, weights):
    return jnp.concatenate(
        [jnp.dot(gathered, weight, preferred_element_type=jnp.float32) for weight in weights], 1
    )


def attend(query_sum, key_value, positions, own_segment, segments):
    row_count = query_sum.shape[0]
    head_width = key_value.shape[1] // 2
    heads_here = query_sum.shape[1] // head_width
    query = rotate(query_sum.reshape(row_count, heads_here, head_width), positions[:, None]).astype(
        jnp.bfloat16
    )
    scores = jnp.einsum(
        "rhd,kd->rhk", query, key_value[:, :head_width], preferred_element_type=jnp.float32
    )
    scores = scores * head_width ** (-0.5)
    key_places = jnp.arange(segments.shape[0]).astype(jnp.float32)
    allowed = (key_places[None, :] <= positions[:, None]) & (
        segments[None, :] == own_segment[:, None]
    )
    expos = jnp.where(allowed[:, None, :], jnp.exp(scores), jnp.float32(0.0))
    probs = (expos / jnp.sum(expos, -1, keepdims=True)).astype(jnp.bfloat16)
    mixed = jnp.einsum(
        "rhk,kd->rhd", probs, key_value[:, head_width:], preferred_element_type=jnp.float32
    )
    return mixed.astype(jnp.bfloat16).reshape(row_count, heads_here * head_width)


def per_device(activations, ln_gain, segments, w_query, w_key_value, w_gate, w_up, w_out, w_down):
    values_f = activations.astype(jnp.float32)
    row_mean = lax.psum(jnp.sum(values_f, 1), "hid") / D
    centered = values_f - row_mean[:, None]
    variance = lax.psum(jnp.sum(centered * centered, 1), "hid") / D
    normed = (centered * lax.rsqrt(variance + EPSILON)[:, None] * ln_gain).astype(jnp.bfloat16)
    gathered = lax.all_gather(normed, "ffn", axis=0, tiled=True)
    row_count = gathered.shape[0] // lax.axis_size("hid")
    first_own = lax.axis_index("hid") * row_count
    positions = (first_own + jnp.arange(row_count)).astype(jnp.float32)
    own_segment = lax.dynamic_slice_in_dim(segments, first_own, row_count, 0)
    query_width = w_query.shape[1]
    unit_width = w_gate.shape[1]
    all_places = jnp.arange(gathered.shape[0]).astype(jnp.float32)
    pair_sums = lax.psum(
        jnp.dot(gathered, w_key_value, preferred_element_type=jnp.float32).astype(jnp.bfloat16),
        "hid",
    ).astype(jnp.float32)
    key_value = finish_pairs(pair_sums, all_places)
    query_weights = [w_query]
    query_part = lax.psum_scatter(
        row_products(gathered, query_weights + [w_gate, w_up]).astype(jnp.bfloat16),
        "hid",
        scatter_dimension=0,
        tiled=True,
    ).astype(jnp.float32)
    attention = attend(query_part[:, :query_width], key_value, positions, own_segment, segments)
    gate_sum = query_part[
        :, query_part.shape[1] - 2 * unit_width : query_part.shape[1] - unit_width
    ]
    up_sum = query_part[:, query_part.shape[1] - unit_width :]
    hidden = (jax.nn.silu(gate_sum) * up_sum).astype(jnp.bfloat16)
    combined = jnp.concatenate([attention, hidden], 1)
    slab_rows = lax.all_gather(combined, "hid", axis=0, tiled=True)
    head_term = jnp.dot(slab_rows[:, :query_width], w_out, preferred_element_type=jnp.float32)
    partial_out = head_term + jnp.dot(
        slab_rows[:, query_width:], w_down, preferred_element_type=jnp.float32
    )
    output_sum = lax.psum_scatter(
        partial_out.astype(jnp.bfloat16), "ffn", scatter_dimension=0, tiled=True
    ).astype(jnp.float32)
    return (values_f + output_sum).astype(jnp.bfloat16)


def solution(mesh):
    placed = (
        P("ffn", "hid"),
        P("hid"),
        P(),
        P("hid", "ffn"),
        P("hid", None),
        P("hid", "ffn"),
        P("hid", "ffn"),
        P("ffn", "hid"),
        P("ffn", "hid"),
    )
    return jax.shard_map(
        per_device, mesh=mesh, in_specs=placed, out_specs=P("ffn", "hid"), check_vma=False
    )
```

profile of v0, /device:TPU:32, one launch (start us, length us, event | category | flops | bytes accessed | tf_op | source)
XLA Modules:
  0.0 469.8 jit_solution(2877936539196751146)
XLA Ops:
  6.5 1.1 convert_reduce_fusion
  7.7 40.7 %psum.21 = f32[64]{0:T(128)S(1)} all-reduce(f32[64]{0:T(128)S(1)} %convert_reduce_fusion), channel_id=1, replica_groups=mesh['hid'=16,'ffn'=16] {'hid'}, use_global_device_ids=true, to_apply=%region_1.0 | all-reduce | flops 64 | bytes 512 | tf_op jit(solution)/shard_map/psum | solution.py:62
  48.4 1.1 fusion.21
  49.4 35.5 %psum.22 = f32[64]{0:T(128)S(1)} all-reduce(f32[64]{0:T(128)S(1)} %fusion.21), channel_id=1, replica_groups=mesh['hid'=16,'ffn'=16] {'hid'}, use_global_device_ids=true, to_apply=%region_3.0 | all-reduce | flops 64 | bytes 512 | tf_op jit(solution)/shard_map/psum | solution.py:64
  84.9 1.6 fusion.23
  86.6 37.5 %all-gather.3.cloned.1.call-done = bf16[1024,640]{1,0:T(8,128)(2,1)} async-done(((bf16[64,640]{1,0:T(8,128)(2,1)}), bf16[1024,640]{1,0:T(8,128)(2,1)}) %all-gather.3.cloned.1.call-update) | async-done | bytes 1310736 | tf_op jit(solution)/shard_map/all_gather | solution.py:66
  124.1 3.5 convolution_convert_fusion.3
  127.7 7.3 %convolution_convert_fusion = bf16[1024,2304]{1,0:T(8,128)(2,1)} fusion(bf16[1024,640]{1,0:T(8,128)(2,1)} %all-gather.3.cloned.1.call-done, bf16[640,2304]{1,0:T(8,128)(2,1)S(1)} %copy-done), kind=kOutput, calls=%fused_computation.1 | convolution fusion | flops 3022258176 | bytes 8978432 | tf_op jit(solution)/shard_map/dot_general | solution.py:33
  134.9 5.4 %convolution_convert_fusion.1 = bf16[1024,2304]{1,0:T(8,128)(2,1)} fusion(bf16[1024,640]{1,0:T(8,128)(2,1)S(1)} %copy-done.4, bf16[640,2304]{1,0:T(8,128)(2,1)S(1)} %copy-done.3), kind=kOutput, calls=%fused_computation.2 | convolution fusion | flops 3022258176 | bytes 8978432 | tf_op jit(solution)/shard_map/dot_general | solution.py:33
  140.4 2.6 convolution_convert_fusion.2
  143.0 2.6 copy.14
  145.6 9.9 %pad_maximum_fusion = bf16[1024,5376]{1,0:T(8,128)(2,1)} fusion(bf16[1024,2304]{1,0:T(8,128)(2,1)} %convolution_convert_fusion, bf16[1024,2304]{1,0:T(8,128)(2,1)} %convolution_convert_fusion.1, bf16[1024,768]{1,0:T(8,128)(2,1)} %copy.14), kind=kLoop, calls=%fused_computation | loop fusion | flops 33030144 | bytes 22020096 | tf_op jit(solution)/shard_map/concatenate | solution.py:32
  156.6 67.5 %all-reduce.2.cloned.1.call-done = bf16[1024,512]{1,0:T(8,128)(2,1)} async-done(((bf16[1024,512]{1,0:T(8,128)(2,1)}), bf16[1024,512]{1,0:T(8,128)(2,1)}) %all-reduce.2.cloned.1.call-update) | async-done | bytes 1048592 | tf_op jit(solution)/shard_map/psum | solution.py:74
  224.1 1.5 convert_element_type.73
  225.6 3.1 fusion.12
  228.7 94.4 %reduce-scatter.3.cloned.1.call-done = bf16[64,5376]{1,0:T(8,128)(2,1)} async-done(((bf16[1024,5376]{1,0:T(8,128)(2,1)}), bf16[64,5376]{1,0:T(8,128)(2,1)}) %reduce-scatter.3.cloned.1.call-update) | async-done | bytes 688144 | tf_op jit(solution)/shard_map/reduce_scatter | solution.py:80
  324.3 2.3 fusion.4
  326.6 1.8 fusion.5
  328.4 1.2 convert_element_type.71
  330.7 65.8 %all-gather.5.cloned.1.call-done = bf16[1024,3072]{1,0:T(8,128)(2,1)} async-done(((bf16[64,3072]{1,0:T(8,128)(2,1)}), bf16[1024,3072]{1,0:T(8,128)(2,1)}) %all-gather.5.cloned.1.call-update) | async-done | bytes 6291472 | tf_op jit(solution)/shard_map/all_gather | solution.py:93
  396.4 6.6 %fusion = f32[1024,640]{1,0:T(8,128)S(1)} fusion(bf16[2304,640]{1,0:T(8,128)(2,1)} %param.17, bf16[1024,3072]{1,0:T(8,128)(2,1)} %all-gather.5.cloned.1.call-done), kind=kOutput, calls=%fused_computation.3 | convolution fusion | flops 3019898880 | bytes 10289152 | tf_op jit(solution)/shard_map/dot_general | solution.py:95
  403.1 4.0 add_convert_fusion
  407.1 54.6 %reduce-scatter.5.cloned.1.call-done = bf16[64,640]{1,0:T(8,128)(2,1)} async-done(((bf16[1024,640]{1,0:T(8,128)(2,1)}), bf16[64,640]{1,0:T(8,128)(2,1)}) %reduce-scatter.5.cloned.1.call-update) | async-done | bytes 81936 | tf_op jit(solution)/shard_map/reduce_scatter | solution.py:98
  461.7 1.5 fusion.24
  (39 shorter events, 3.3 us)
Async XLA Ops:
  6.5 121.1 %copy-start = (bf16[640,2304]{1,0:T(8,128)(2,1)S(1)}, bf16[640,2304]{1,0:T(8,128)(2,1)}, u32[]{:S(2)}) copy-start(bf16[640,2304]{1,0:T(8,128)(2,1)} %param.15) | copy-start | bytes 8847364
  6.5 117.6 %all-gather.3.cloned.1.call-start = ((), (), s32[]{:S(2)}) async-start(), calls=%async_computation.2 | async-start | bytes 1392640 | tf_op jit(solution)/shard_map/all_gather | solution.py:66
  86.6 137.6 %all-reduce.2.cloned.1.call-start = ((), (), s32[]{:S(2)}) async-start(), calls=%async_computation.4 | async-start | bytes 2097152 | tf_op jit(solution)/shard_map/psum | solution.py:74
  127.6 195.6 %reduce-scatter.3.cloned.1.call-start = ((), (), s32[]{:S(2)}) async-start(), calls=%async_computation.3 | async-start | bytes 11698176 | tf_op jit(solution)/shard_map/reduce_scatter | solution.py:80
  127.6 7.3 %copy-start.3 = (bf16[640,2304]{1,0:T(8,128)(2,1)S(1)}, bf16[640,2304]{1,0:T(8,128)(2,1)}, u32[]{:S(2)}) copy-start(bf16[640,2304]{1,0:T(8,128)(2,1)} %param.14) | copy-start | bytes 8847364
  127.7 7.3 %copy-start.4 = (bf16[1024,640]{1,0:T(8,128)(2,1)S(1)}, bf16[1024,640]{1,0:T(8,128)(2,1)}, u32[]{:S(2)}) copy-start(bf16[1024,640]{1,0:T(8,128)(2,1)} %all-gather.3.cloned.1.call-done) | copy-start | bytes 3932164
  134.9 5.4 %copy-start.5 = (bf16[640,768]{1,0:T(8,128)(2,1)S(1)}, bf16[640,768]{1,0:T(8,128)(2,1)}, u32[]{:S(2)}) copy-start(bf16[640,768]{1,0:T(8,128)(2,1)} %param.12) | copy-start | bytes 2949124
  155.5 0.7 copy-start.2
  155.5 240.9 %all-gather.5.cloned.1.call-start = ((), (), s32[]{:S(2)}) async-start(), calls=%async_computation.5 | async-start | bytes 6684672 | tf_op jit(solution)/shard_map/all_gather | solution.py:93
  330.6 131.1 %reduce-scatter.5.cloned.1.call-start = ((), (), s32[]{:S(2)}) async-start(), calls=%async_computation.6 | async-start | bytes 1392640 | tf_op jit(solution)/shard_map/reduce_scatter | solution.py:98
  396.4 6.7 %copy-start.6 = (bf16[768,640]{1,0:T(8,128)(2,1)S(1)}, bf16[768,640]{1,0:T(8,128)(2,1)}, u32[]{:S(2)}) copy-start(bf16[768,640]{1,0:T(8,128)(2,1)} %param.16) | copy-start | bytes 2949124
  403.1 58.6 %copy-start.1 = (bf16[64,640]{1,0:T(8,128)(2,1)S(1)}, bf16[64,640]{1,0:T(8,128)(2,1)}, u32[]{:S(2)}) copy-start(bf16[64,640]{1,0:T(8,128)(2,1)} %param.9) | copy-start | bytes 245764
Sparse Core Ops, SparseCore 0:
  86.7 37.3 all-gather.2
  127.7 96.3 all-reduce.1
  227.9 95.2 reduce-scatter.2
  330.7 65.6 all-gather.4
  407.2 54.4 reduce-scatter.4
where the time goes:
time: 474 us; the launch traced here: 470 us
  waiting for transfers between devices  320 us (68%)
  blocking collectives  76.1 us (16%)
  matrix products  33.5 us (7%)
  other arithmetic  22.4 us (5%)
  between operations  13.3 us (3%)
    reduce_scatter x1, waiting for transfers between devices, per_device(): lax.psum_scatter(row_products(gathered, query_weights + [w_gate, w_up]).a...  94.4 us
    psum x1, waiting for transfers between devices, per_device(): lax.psum(jnp.dot(gathered, w_key_value, preferred_element_type=jnp.float3...  67.5 us
    all_gather x1, waiting for transfers between devices, per_device(): slab_rows = lax.all_gather(combined, 'hid', axis=0, tiled=True)  65.8 us
    reduce_scatter x1, waiting for transfers between devices, per_device(): lax.psum_scatter(partial_out.astype(jnp.bfloat16), 'ffn', scatter_dimensi...  54.6 us
    psum x1, blocking collectives, per_device(): row_mean = lax.psum(jnp.sum(values_f, 1), 'hid') / D  40.7 us
    all_gather x1, waiting for transfers between devices, per_device(): gathered = lax.all_gather(normed, 'ffn', axis=0, tiled=True)  37.5 us
    psum x1, blocking collectives, per_device(): variance = lax.psum(jnp.sum(centered * centered, 1), 'hid') / D  35.5 us
    dot_general x3, matrix products, row_products(): jnp.dot(gathered, weight, preferred_element_type=jnp.float32)  15.3 us
  transfers between devices with their start and end apart: 5, of which 5 were waited for; matrix products, arithmetic and copies ran while one was open for 7% of the time, Pallas kernels for 0%

commit v1 on v0

v1 whole, which is shorter than its diff:
```python
import jax
import jax.numpy as jnp
import numpy as np
from jax import lax
from jax.experimental import pallas as pl
from jax.experimental.pallas import tpu as pltpu
from jax.sharding import PartitionSpec as P

D = 10240
HEAD = 256
TOKENS = 1024
EPSILON = 1e-06

SIDE = 4
RING = 8
GROUP = SIDE * SIDE
ROWS = TOKENS // GROUP
FEATS = D // GROUP
WIDE = 384
STEPS = 7
UNITS = 8
HALF = ROWS // 2
QUARTER = ROWS // 4
F32 = jnp.float32
BF16 = jnp.bfloat16


def tables():
    half = HEAD // 2
    frequency = np.float32(10000.0) ** (-np.arange(half, dtype=np.float32) / np.float32(half))
    angles = np.arange(TOKENS, dtype=np.float32)[:, None] * frequency[None, :].astype(np.float32)
    wide = angles.astype(np.float64)
    return np.stack([np.cos(wide), np.sin(wide)]).astype(np.float32)


def block_kernel(
    act,
    gain,
    seg,
    table,
    w_query,
    w_pairs,
    w_gate,
    w_up,
    w_out,
    w_down,
    out,
    w_in,
    w_back,
    w_kv,
    turn,
    stat,
    stat_in,
    rows_all,
    pair_part,
    pair_in,
    pair_sum,
    pair_all,
    kv_all,
    part,
    land1,
    land2,
    mixed,
    total,
    sib_out,
    sib_in,
    ring_out,
    ring_half,
    ring_in,
    w_sem,
    wb_sem,
    m_sem,
    small_s,
    small_r,
    zx_s,
    zx_r,
    zk_s,
    zk_r,
    rs_s,
    rs_r,
    ag_s,
    ag_r,
    zr_s,
    zr_r,
):
    hid = lax.axis_index("hid")
    ffn = lax.axis_index("ffn")
    x, y = hid // SIDE, hid % SIDE
    z, core = ffn // 2, ffn % 2

    def mod4(v):
        return (v + SIDE) % SIDE

    def mod8(v):
        return (v + RING) % RING

    def dev_x(d):
        return (mod4(x + d) * SIDE + y, ffn)

    def dev_y(d):
        return (x * SIDE + mod4(y + d), ffn)

    def dev_z(d):
        return (hid, mod8(z + d) * 2 + core)

    sibling = (hid, z * 2 + 1 - core)
    dirs = (1, -1)
    orders = ((x, y, dev_x, dev_y), (y, x, dev_y, dev_x))

    def remote(src, dst, ssem, rsem, dev):
        return pltpu.make_async_remote_copy(
            src_ref=src,
            dst_ref=dst,
            send_sem=ssem,
            recv_sem=rsem,
            device_id=dev,
            device_id_type=pl.DeviceIdType.MESH,
        )

    def w_copy(s, o):
        if s == 0:
            src = w_query.at[:, pl.ds(o * WIDE, WIDE)]
        else:
            src = (w_gate, w_up)[o].at[:, pl.ds((s - 1) * WIDE, WIDE)]
        return pltpu.make_async_copy(src, w_in.at[s, o], w_sem.at[s, o])

    def wb_copy(u):
        if u < 2:
            src = w_out.at[pl.ds(u * WIDE, WIDE)]
        else:
            src = w_down.at[pl.ds((u - 2) * WIDE, WIDE)]
        return pltpu.make_async_copy(src, w_back.at[u], wb_sem.at[u])

    def turn_copy(k, i):
        first = (hid if k == 0 else ffn) * ROWS
        return pltpu.make_async_copy(
            table.at[i, pl.ds(first, ROWS)], turn.at[k, i], m_sem.at[1 + 2 * k + i]
        )

    kv_copy = pltpu.make_async_copy(w_pairs, w_kv, m_sem.at[0])
    kv_copy.start()
    for k in range(2):
        for i in range(2):
            turn_copy(k, i).start()
    for s in range(STEPS):
        for o in range(2):
            w_copy(s, o).start()
    for u in range(UNITS):
        wb_copy(u).start()

    barrier = pltpu.get_barrier_semaphore()
    partners = [dev_x(d) for d in (1, 2, 3)] + [dev_y(d) for d in (1, 2, 3)]
    partners += [dev_z(1), dev_z(-1), sibling]
    for dev in partners:
        pl.semaphore_signal(barrier, inc=1, device_id=dev, device_id_type=pl.DeviceIdType.MESH)
    pl.semaphore_wait(barrier, len(partners))

    def stat_copy(a, d):
        return remote(
            stat.at[a], stat_in.at[a, d - 1], small_s.at[a, d - 1], small_r.at[a, d - 1],
            (dev_x, dev_y)[a](d),
        )

    def pair_copy(k, d):
        if k == 0:
            src, dst, dev = pair_part.at[mod4(x + d)], pair_in.at[0, d - 1], dev_x(d)
        elif k == 1:
            src, dst, dev = pair_sum, pair_in.at[1, d - 1], dev_y(d)
        else:
            src, dst, dev = pair_all.at[x], pair_all.at[x], dev_x(d)
        return remote(src, dst, small_s.at[2 + k, d - 1], small_r.at[2 + k, d - 1], dev)

    def each(fn, k, what):
        for d in (1, 2, 3):
            getattr(fn(k, d), what)()

    def z_copy(buf, sems, j, i):
        d = dirs[i]
        block = mod8(z - (j - 1) * d) * 2 + core
        ref = buf.at[block] if j < 4 else buf.at[block, pl.ds(i * HALF, HALF)]
        return remote(ref, ref, sems[0].at[j - 1, i], sems[1].at[j - 1, i], dev_z(d))

    def sib_copy(buf, sems, off):
        ref = buf.at[mod8(z + off) * 2 + core]
        row = 4 + (off + 3) // 2
        col = (off + 3) % 2
        return remote(ref, ref, sems[0].at[row, col], sems[1].at[row, col], sibling)

    def z_start(buf, sems):
        for i in range(2):
            z_copy(buf, sems, 1, i).start()
        sib_copy(buf, sems, 0).start()

    def z_step(buf, sems, j):
        if j < 4:
            for i in range(2):
                z_copy(buf, sems, j, i).wait()
                z_copy(buf, sems, j + 1, i).start()
                sib_copy(buf, sems, -j * dirs[i]).start()
        else:
            for i in range(2):
                z_copy(buf, sems, j, i).wait()
            sib_copy(buf, sems, 4).start()
            for off in (0, 1, -1, 2, -2, 3, -3, 4):
                sib_copy(buf, sems, off).wait()

    values = act[...].astype(F32)
    mean = jnp.mean(values, 1, keepdims=True)
    square = jnp.sum((values - mean) ** 2, 1, keepdims=True)
    lane = lax.broadcasted_iota(jnp.int32, (ROWS, 128), 1)
    for a, count in ((0, FEATS), (1, FEATS * SIDE)):
        stat[a] = jnp.where(lane < 64, mean, square)
        each(stat_copy, a, "start")
        if a == 0:
            total[...] = jnp.zeros_like(total)
        each(stat_copy, a, "wait")
        means = [mean] + [stat_in[a, d, :, 0:1] for d in range(3)]
        squares = [square] + [stat_in[a, d, :, 64:65] for d in range(3)]
        mean = (means[0] + means[1] + means[2] + means[3]) * 0.25
        square = squares[0] + squares[1] + squares[2] + squares[3]
        for one in means:
            square += count * (one - mean) ** 2
    scale = lax.rsqrt(square * (1.0 / D) + EPSILON)
    values = act[...].astype(F32)
    normed = ((values - mean) * scale * gain[...]).astype(BF16)
    rows_all[ffn] = normed
    zx = (zx_s, zx_r)
    zk = (zk_s, zk_r)
    z_start(rows_all, zx)

    kv_copy.wait()
    pairs = jnp.dot(normed, w_kv[...], preferred_element_type=F32).astype(BF16)
    for q in range(4):
        pair_part[q] = pairs[:, q * 128 : (q + 1) * 128]
    each(pair_copy, 0, "start")
    z_step(rows_all, zx, 1)
    each(pair_copy, 0, "wait")
    pair_sum[...] = (
        pair_part[x].astype(F32)
        + pair_in[0, 0].astype(F32)
        + pair_in[0, 1].astype(F32)
        + pair_in[0, 2].astype(F32)
    ).astype(BF16)
    each(pair_copy, 1, "start")
    z_step(rows_all, zx, 2)
    each(pair_copy, 1, "wait")
    pair_all[x] = (
        pair_sum[...].astype(F32)
        + pair_in[1, 0].astype(F32)
        + pair_in[1, 1].astype(F32)
        + pair_in[1, 2].astype(F32)
    ).astype(BF16)
    each(pair_copy, 2, "start")
    z_step(rows_all, zx, 3)
    each(pair_copy, 2, "wait")
    for k in range(2):
        for i in range(2):
            turn_copy(k, i).wait()
    first, second = pair_all[0].astype(F32), pair_all[1].astype(F32)
    kv_all[ffn, :, 0:128] = (first * turn[1, 0] - second * turn[1, 1]).astype(BF16)
    kv_all[ffn, :, 128:256] = (first * turn[1, 1] + second * turn[1, 0]).astype(BF16)
    kv_all[ffn, :, 256:384] = pair_all[2]
    kv_all[ffn, :, 384:512] = pair_all[3]
    z_step(rows_all, zx, 4)

    for s in range(STEPS):
        for o in range(2):
            w_copy(s, o).wait()
    for u in range(UNITS):
        wb_copy(u).wait()

    def first_ref(s, o, i, m):
        p1 = orders[o][0]
        d = dirs[i]
        if m == 0:
            return part.at[s, o, mod4(p1 + 2), pl.ds(2 * i, 2)]
        if m == 1:
            return part.at[s, o, mod4(p1 + d), pl.ds(2 * (1 - i), 2)]
        return part.at[s, o, mod4(p1 + d), pl.ds(2 * i, 2)]

    def first_copy(s, o, i, m):
        at = o * 12 + i * 3 + m
        return remote(
            first_ref(s, o, i, m), land1.at[s, o, i, m], rs_s.at[s, at], rs_r.at[s, at],
            orders[o][2](dirs[i]),
        )

    def second_ref(s, o, i, m):
        p1, p2 = orders[o][0], orders[o][1]
        d = dirs[i]
        if m == 0:
            return part.at[s, o, p1, mod4(p2 + 2), pl.ds(i * HALF, HALF)]
        if m == 1:
            return part.at[s, o, p1, mod4(p2 + d), pl.ds((1 - i) * HALF, HALF)]
        return part.at[s, o, p1, mod4(p2 + d), pl.ds(i * HALF, HALF)]

    def second_copy(s, o, i, m):
        at = o * 12 + 6 + i * 3 + m
        return remote(
            second_ref(s, o, i, m), land2.at[s, o, i, m], rs_s.at[s, at], rs_r.at[s, at],
            orders[o][3](dirs[i]),
        )

    both = [(o, i) for o in range(2) for i in range(2)]

    def phase0(s):
        for o in range(2):

            def tile(t, carry):
                rows = rows_all[pl.ds(t * SIDE, SIDE)].reshape(SIDE * ROWS, FEATS)
                res = jnp.dot(rows, w_in[s, o], preferred_element_type=F32).astype(BF16)
                res = res.reshape(SIDE, ROWS, WIDE)
                if o == 0:
                    part[s, 0, t] = res
                else:
                    part[s, 1, :, t] = res
                return carry

            lax.fori_loop(0, SIDE, tile, 0)
            for i in range(2):
                first_copy(s, o, i, 0).start()
            for i in range(2):
                first_copy(s, o, i, 1).start()

    def add_into(ref, land):
        ref[...] = (ref[...].astype(F32) + land[...].astype(F32)).astype(BF16)

    def phase1(s):
        for o, i in both:
            first_copy(s, o, i, 0).wait()
            add_into(first_ref(s, o, i, 2), land1.at[s, o, i, 0])
            first_copy(s, o, i, 2).start()

    def phase2(s):
        for o in range(2):
            p1 = orders[o][0]
            for i in range(2):
                first_copy(s, o, i, 1).wait()
                first_copy(s, o, i, 2).wait()
            for i in range(2):
                ref = part.at[s, o, p1, pl.ds(2 * i, 2)]
                ref[...] = (
                    ref[...].astype(F32)
                    + land1[s, o, i, 2].astype(F32)
                    + land1[s, o, 1 - i, 1].astype(F32)
                ).astype(BF16)
            for i in range(2):
                second_copy(s, o, i, 0).start()
                second_copy(s, o, i, 1).start()

    def phase3(s):
        for o, i in both:
            second_copy(s, o, i, 0).wait()
            add_into(second_ref(s, o, i, 2), land2.at[s, o, i, 0])
            second_copy(s, o, i, 2).start()

    def attend(left, right):
        seg_row = seg[...].astype(F32)
        key_at = lax.broadcasted_iota(jnp.int32, (ROWS, TOKENS), 1)
        row_at = lax.broadcasted_iota(jnp.int32, (ROWS, TOKENS), 0) + hid * ROWS
        own = jnp.sum(jnp.where(key_at == row_at, seg_row, 0.0), 1, keepdims=True)
        allowed = (key_at <= row_at) & (seg_row == own)
        keys = kv_all[:, :, 0:HEAD].reshape(TOKENS, HEAD)
        vals = kv_all[:, :, HEAD : 2 * HEAD].reshape(TOKENS, HEAD)
        cosine, sine = turn[0, 0], turn[0, 1]
        groups = [v[:, k * 128 : (k + 1) * 128] for v in (left, right) for k in range(3)]
        pieces = []
        for h in range(3):
            a, b = groups[2 * h], groups[2 * h + 1]
            query = jnp.concatenate([a * cosine - b * sine, a * sine + b * cosine], 1).astype(BF16)
            scores = lax.dot_general(
                query, keys, (((1,), (1,)), ((), ())), preferred_element_type=F32
            ) * (HEAD**-0.5)
            expos = jnp.where(allowed, jnp.exp(scores), 0.0)
            probs = (expos / jnp.sum(expos, 1, keepdims=True)).astype(BF16)
            res = jnp.dot(probs, vals, preferred_element_type=F32).astype(BF16)
            pieces += [res[:, 0:128], res[:, 128:256]]
        return jnp.concatenate(pieces[:3], 1), jnp.concatenate(pieces[3:], 1)

    def put(u, block):
        mixed[u, 0, y, x] = block[0:HALF]
        mixed[u, 1, x, y] = block[HALF:ROWS]

    def gather_copy(u, o, k, i):
        p1, p2, dev1, dev2 = orders[o]
        d = dirs[i]
        if k == 0:
            ref, dev = mixed.at[u, o, p2, p1], dev1(d)
        elif k == 1:
            ref, dev = mixed.at[u, o, p2, mod4(p1 - d), pl.ds(i * QUARTER, QUARTER)], dev1(d)
        elif k == 2:
            ref, dev = mixed.at[u, o, p2], dev2(d)
        else:
            ref, dev = mixed.at[u, o, mod4(p2 - d), pl.ds(2 * i, 2)], dev2(d)
        at = o * 8 + k * 2 + i
        return remote(ref, ref, ag_s.at[u, at], ag_r.at[u, at], dev)

    def phase4(s):
        sums = []
        for o in range(2):
            p1, p2 = orders[o][0], orders[o][1]
            for i in range(2):
                second_copy(s, o, i, 1).wait()
                second_copy(s, o, i, 2).wait()
            sums.append(
                jnp.concatenate(
                    [
                        part[s, o, p1, p2, i * HALF : (i + 1) * HALF].astype(F32)
                        + land2[s, o, i, 2].astype(F32)
                        + land2[s, o, 1 - i, 1].astype(F32)
                        for i in range(2)
                    ],
                    0,
                )
            )

        @pl.when(s == 0)
        def _():
            left, right = attend(*sums)
            put(0, left)
            put(1, right)
            for u in range(2):
                for o, i in both:
                    gather_copy(u, o, 0, i).start()

        @pl.when(s > 0)
        def _():
            gate, up = sums
            put(s + 1, (gate / (1.0 + jnp.exp(-gate)) * up).astype(BF16))
            for o, i in both:
                gather_copy(s + 1, o, 0, i).start()

    def phase5(u):
        for o, i in both:
            gather_copy(u, o, 0, i).wait()
            gather_copy(u, o, 1, i).start()

    def phase6(u):
        for o in range(2):
            for i in range(2):
                gather_copy(u, o, 1, i).wait()
            for i in range(2):
                gather_copy(u, o, 2, i).start()

    def phase7(u):
        for o, i in both:
            gather_copy(u, o, 2, i).wait()
            gather_copy(u, o, 3, i).start()

    def phase8(u):
        for o in range(2):
            for i in range(2):
                gather_copy(u, o, 3, i).wait()
            for p in range(2):
                rows = mixed[u, o, 2 * p : 2 * p + 2].reshape(2 * SIDE * HALF, WIDE)
                total[o, p * 256 : (p + 1) * 256] += jnp.dot(
                    rows, w_back[u], preferred_element_type=F32
                )

    def slot(t, carry):
        for k, fn in enumerate((phase0, phase1, phase2, phase3)):
            s = t - k
            pl.when((s >= 0) & (s < STEPS))(lambda fn=fn, s=s: fn(s))

        @pl.when(t == 0)
        def _():
            z_start(kv_all, zk)

        for j in range(1, 5):
            pl.when(t == j)(lambda j=j: z_step(kv_all, zk, j))

        s4 = t - 4
        pl.when((s4 >= 0) & (s4 < STEPS))(lambda: phase4(s4))

        for k, fn in ((5, phase5), (6, phase6), (7, phase7), (8, phase8)):
            s = t - k

            @pl.when((s >= 0) & (s < STEPS))
            def _(fn=fn, s=s):
                def unit(u, c):
                    fn(u)
                    return c

                lax.fori_loop(jnp.where(s == 0, 0, s + 1), s + 2, unit, 0)

        return carry

    lax.fori_loop(0, STEPS + 8, slot, 0)

    offsets = (4, 3, -3, 2, -2, 1, -1, 0)

    def block_rows(block):
        bx, by = block // SIDE, block % SIDE
        one = total[0, pl.ds(pl.multiple_of((by * SIDE + bx) * HALF, HALF), HALF)]
        two = total[1, pl.ds(pl.multiple_of(block * HALF, HALF), HALF)]
        return jnp.concatenate([one, two], 0)

    def sib_sum(k):
        at = mod8(z + offsets[k])
        return remote(sib_out.at[at], sib_in.at[at], zr_s.at[k], zr_r.at[k], sibling)

    for k in range(RING):
        at = mod8(z + offsets[k])
        sib_out[at] = block_rows(at * 2 + 1 - core).astype(BF16)
        sib_sum(k).start()

    def chip_sum(k):
        at = mod8(z + offsets[k])
        sib_sum(k).wait()
        return block_rows(at * 2 + core) + sib_in[at].astype(F32)

    def half_copy(i):
        return remote(
            ring_out.at[0, i, pl.ds(0, HALF)], ring_half.at[i], zr_s.at[8 + i], zr_r.at[8 + i],
            dev_z(dirs[i]),
        )

    def full_copy(j, i):
        at = 10 + 2 * j + i
        return remote(
            ring_out.at[1 + j, i], ring_in.at[j, i], zr_s.at[at], zr_r.at[at], dev_z(dirs[i])
        )

    far = chip_sum(0)
    for i in range(2):
        ring_out[0, i, 0:HALF] = far[i * HALF : (i + 1) * HALF].astype(BF16)
        half_copy(i).start()
    for i in range(2):
        here = chip_sum(1 + i)
        half_copy(i).wait()
        come = ring_half[i].astype(F32)
        pad = jnp.zeros((HALF, FEATS), F32)
        come = jnp.concatenate([come, pad] if i == 0 else [pad, come], 0)
        ring_out[1, i] = (here + come).astype(BF16)
        full_copy(0, i).start()
    for j in (1, 2):
        for i in range(2):
            here = chip_sum(1 + 2 * j + i)
            full_copy(j - 1, i).wait()
            ring_out[1 + j, i] = (here + ring_in[j - 1, i].astype(F32)).astype(BF16)
            full_copy(j, i).start()
    here = chip_sum(7) + act[...].astype(F32)
    for i in range(2):
        full_copy(2, i).wait()
        here += ring_in[2, i].astype(F32)
    out[...] = here.astype(BF16)


def per_device(activations, ln_gain, segments, w_query, w_key_value, w_gate, w_up, w_out, w_down):
    vmem = pl.BlockSpec(memory_space=pltpu.VMEM)
    anywhere = pl.BlockSpec(memory_space=pl.ANY)
    dma = pltpu.SemaphoreType.DMA
    scratch = [
        pltpu.VMEM((STEPS, 2, FEATS, WIDE), BF16),
        pltpu.VMEM((UNITS, WIDE, FEATS), BF16),
        pltpu.VMEM((FEATS, 512), BF16),
        pltpu.VMEM((2, 2, ROWS, 128), F32),
        pltpu.VMEM((2, ROWS, 128), F32),
        pltpu.VMEM((2, 3, ROWS, 128), F32),
        pltpu.VMEM((GROUP, ROWS, FEATS), BF16),
        pltpu.VMEM((4, ROWS, 128), BF16),
        pltpu.VMEM((2, 3, ROWS, 128), BF16),
        pltpu.VMEM((ROWS, 128), BF16),
        pltpu.VMEM((4, ROWS, 128), BF16),
        pltpu.VMEM((GROUP, ROWS, 512), BF16),
        pltpu.VMEM((STEPS, 2, SIDE, SIDE, ROWS, WIDE), BF16),
        pltpu.VMEM((STEPS, 2, 2, 3, 2, ROWS, WIDE), BF16),
        pltpu.VMEM((STEPS, 2, 2, 3, HALF, WIDE), BF16),
        pltpu.VMEM((UNITS, 2, SIDE, SIDE, HALF, WIDE), BF16),
        pltpu.VMEM((2, GROUP * HALF, FEATS), F32),
        pltpu.VMEM((RING, ROWS, FEATS), BF16),
        pltpu.VMEM((RING, ROWS, FEATS), BF16),
        pltpu.VMEM((4, 2, ROWS, FEATS), BF16),
        pltpu.VMEM((2, HALF, FEATS), BF16),
        pltpu.VMEM((3, 2, ROWS, FEATS), BF16),
        dma((STEPS, 2)),
        dma((UNITS,)),
        dma((5,)),
        dma((5, 3)),
        dma((5, 3)),
        dma((8, 2)),
        dma((8, 2)),
        dma((8, 2)),
        dma((8, 2)),
        dma((STEPS, 24)),
        dma((STEPS, 24)),
        dma((UNITS, 16)),
        dma((UNITS, 16)),
        dma((16,)),
        dma((16,)),
    ]
    return pl.pallas_call(
        block_kernel,
        out_shape=jax.ShapeDtypeStruct((ROWS, FEATS), BF16),
        in_specs=[vmem, vmem, vmem] + [anywhere] * 7,
        out_specs=vmem,
        scratch_shapes=scratch,
        compiler_params=pltpu.CompilerParams(
            collective_id=0, has_side_effects=True, vmem_limit_bytes=60 * 1024 * 1024
        ),
    )(
        activations,
        ln_gain.reshape(1, FEATS),
        segments.reshape(1, TOKENS),
        jnp.asarray(tables()),
        w_query,
        w_key_value,
        w_gate,
        w_up,
        w_out,
        w_down,
    )


def solution(mesh):
    placed = (
        P("ffn", "hid"),
        P("hid"),
        P(),
        P("hid", "ffn"),
        P("hid", None),
        P("hid", "ffn"),
        P("hid", "ffn"),
        P("ffn", "hid"),
        P("ffn", "hid"),
    )
    return jax.shard_map(
        per_device, mesh=mesh, in_specs=placed, out_specs=P("ffn", "hid"), check_vma=False
    )
```

time: 474 us -> 155 us (0.33)
  waiting for transfers between devices: 320 us -> 0 us
  Pallas kernels: 0 us -> 152 us
  blocking collectives: 76.1 us -> 0 us
  matrix products: 33.5 us -> 0 us
  other arithmetic: 22.4 us -> 0 us
  between operations: 13.3 us -> 0.01 us
    pallas_call x0 -> x1, Pallas kernels: none -> 152 us  [per_device(): pl.pallas_call(block_kernel, out_shape=jax.ShapeDtypeStruct((ROWS, FEATS)...]
    reduce_scatter x2 -> x0, waiting for transfers between devices: 149 us -> none  [the longest x1 94.4 us: per_device(): lax.psum_scatter(row_products(gathered, query_weights + [w_gate, w_up]).a...]
    all_gather x2 -> x0, waiting for transfers between devices: 103 us -> none  [the longest x1 65.8 us: per_device(): slab_rows = lax.all_gather(combined, 'hid', axis=0, tiled=True)]
    psum x2 -> x0, blocking collectives: 76.1 us -> none  [the longest x1 40.7 us: per_device(): row_mean = lax.psum(jnp.sum(values_f, 1), 'hid') / D]
    psum x1 -> x0, waiting for transfers between devices: 67.5 us -> none  [per_device(): lax.psum(jnp.dot(gathered, w_key_value, preferred_element_type=jnp.float3...]
    dot_general x8 -> x0, matrix products: 33.5 us -> none  [the longest x3 15.3 us: row_products(): jnp.dot(gathered, weight, preferred_element_type=jnp.float32)]
    concatenate x2 -> x0, other arithmetic: 10.7 us -> none  [the longest x1 9.89 us: row_products(): jnp.concatenate([jnp.dot(gathered, weight, preferred_element_type=jnp.flo...]
    convert_element_type x7 -> x0, other arithmetic: 6.03 us -> none  [the longest x1 1.62 us: per_device(): (centered * lax.rsqrt(variance + EPSILON)[:, None] * ln_gain).astype(jnp....]
  transfers between devices with their start and end apart: 5 -> 0, of which waited for: 5 -> 0; matrix products, arithmetic and copies ran while one was open for 7% -> 0% of each run, Pallas kernels for 0% -> 0%
where the time goes in v1:
time: 155 us; the launch traced here: 154 us
  Pallas kernels  152 us (98%)
  local copies, waits for them, and re-layouts  2.8 us (2%)
    pallas_call x1, Pallas kernels, per_device(): pl.pallas_call(block_kernel, out_shape=jax.ShapeDtypeStruct((ROWS, FEATS)...  152 us

profile of v1, /device:TPU:32, one launch (start us, length us, event | category | flops | bytes accessed | tf_op | source)
XLA Modules:
  0.0 154.3 jit_solution(7886831719868360127)
XLA Ops:
  0.0 1.3 reshape.6.gain
  1.3 151.5 %shard_map.100 = bf16[64,640]{1,0:T(8,128)(2,1)} custom-call(bf16[64,640]{1,0:T(8,128)(2,1)} %act.1, f32[1,640]{1,0:T(1,128)} %reshape.6.gain, s32[1,1024]{1,0:T(1,128)} %bitcast.1, f32[2,1024,128]{2,1,0:T(8,128)} %constant.2.clone.table, bf16[640,768]{1,0:T(8,128)(2,1)} %w_query.1, bf16[640,512]{1,0:T(8,128)(2,1)} %w_pairs.1, bf16[640,2304]{1,0:T(8,128)(2,1)} %w_gate.1, ...), custom_call_target="tpu_custom_call" | custom-call | tf_op jit(solution)/shard_map/pallas_call | solution.py:592
  152.8 1.5 copy.12

commit v2 on v1

--- a/solution.py
+++ b/solution.py
@@ -59,7 +59,9 @@
     kv_all,
     part,
     land1,
+    last1,
     land2,
+    last2,
     mixed,
     total,
     sib_out,
@@ -94,18 +96,28 @@
     def mod8(v):
         return (v + RING) % RING
 
+    ids_x = {d: mod4(x + d) * SIDE + y for d in (1, 2, 3)}
+    ids_y = {d: x * SIDE + mod4(y + d) for d in (1, 2, 3)}
+    ids_z = {d: mod8(z + d) * 2 + core for d in (1, -1)}
+
     def dev_x(d):
-        return (mod4(x + d) * SIDE + y, ffn)
+        return (ids_x[d % SIDE], ffn)
 
     def dev_y(d):
-        return (x * SIDE + mod4(y + d), ffn)
+        return (ids_y[d % SIDE], ffn)
 
     def dev_z(d):
-        return (hid, mod8(z + d) * 2 + core)
+        return (hid, ids_z[d])
 
     sibling = (hid, z * 2 + 1 - core)
     dirs = (1, -1)
-    orders = ((x, y, dev_x, dev_y), (y, x, dev_y, dev_x))
+    devs = ((dev_x, dev_y), (dev_y, dev_x))
+
+    barrier = pltpu.get_barrier_semaphore()
+    partners = [dev_x(d) for d in (1, 2, 3)] + [dev_y(d) for d in (1, 2, 3)]
+    partners += [dev_z(1), dev_z(-1), sibling]
+    for dev in partners:
+        pl.semaphore_signal(barrier, inc=1, device_id=dev, device_id_type=pl.DeviceIdType.MESH)
 
     def remote(src, dst, ssem, rsem, dev):
         return pltpu.make_async_remote_copy(
@@ -122,7 +134,7 @@
             src = w_query.at[:, pl.ds(o * WIDE, WIDE)]
         else:
             src = (w_gate, w_up)[o].at[:, pl.ds((s - 1) * WIDE, WIDE)]
-        return pltpu.make_async_copy(src, w_in.at[s, o], w_sem.at[s, o])
+        return pltpu.make_async_copy(src, w_in.at[s, :, pl.ds(o * WIDE, WIDE)], w_sem.at[s, o])
 
     def wb_copy(u):
         if u < 2:
@@ -148,11 +160,6 @@
     for u in range(UNITS):
         wb_copy(u).start()
 
-    barrier = pltpu.get_barrier_semaphore()
-    partners = [dev_x(d) for d in (1, 2, 3)] + [dev_y(d) for d in (1, 2, 3)]
-    partners += [dev_z(1), dev_z(-1), sibling]
-    for dev in partners:
-        pl.semaphore_signal(barrier, inc=1, device_id=dev, device_id_type=pl.DeviceIdType.MESH)
     pl.semaphore_wait(barrier, len(partners))
 
     def stat_copy(a, d):
@@ -222,7 +229,7 @@
             square += count * (one - mean) ** 2
     scale = lax.rsqrt(square * (1.0 / D) + EPSILON)
     values = act[...].astype(F32)
-    normed = ((values - mean) * scale * gain[...]).astype(BF16)
+    normed = ((values - mean) * scale * gain[...].reshape(1, FEATS)).astype(BF16)
     rows_all[ffn] = normed
     zx = (zx_s, zx_r)
     zk = (zk_s, zk_r)
@@ -269,90 +276,72 @@
     for u in range(UNITS):
         wb_copy(u).wait()
 
-    def first_ref(s, o, i, m):
-        p1 = orders[o][0]
-        d = dirs[i]
-        if m == 0:
-            return part.at[s, o, mod4(p1 + 2), pl.ds(2 * i, 2)]
-        if m == 1:
-            return part.at[s, o, mod4(p1 + d), pl.ds(2 * (1 - i), 2)]
-        return part.at[s, o, mod4(p1 + d), pl.ds(2 * i, 2)]
-
-    def first_copy(s, o, i, m):
-        at = o * 12 + i * 3 + m
+    far1 = ((12, 8), (20, 8))
+    near1 = ((8, 4), (28, 4))
+    far2 = ((3, 2), (5, 2))
+    near2 = ((2, 1), (7, 1))
+
+    def rs_copy(s, o, k, i):
+        first, size = (far1, near1, far2, near2)[k][i]
+        at = o * 8 + k * 2 + i
         return remote(
-            first_ref(s, o, i, m), land1.at[s, o, i, m], rs_s.at[s, at], rs_r.at[s, at],
-            orders[o][2](dirs[i]),
+            part.at[s, o, pl.ds(first, size)],
+            (land1, last1, land2, last2)[k].at[s, o, i],
+            rs_s.at[s, at],
+            rs_r.at[s, at],
+            devs[o][k // 2](dirs[i]),
         )
 
-    def second_ref(s, o, i, m):
-        p1, p2 = orders[o][0], orders[o][1]
-        d = dirs[i]
-        if m == 0:
-            return part.at[s, o, p1, mod4(p2 + 2), pl.ds(i * HALF, HALF)]
-        if m == 1:
-            return part.at[s, o, p1, mod4(p2 + d), pl.ds((1 - i) * HALF, HALF)]
-        return part.at[s, o, p1, mod4(p2 + d), pl.ds(i * HALF, HALF)]
-
-    def second_copy(s, o, i, m):
-        at = o * 12 + 6 + i * 3 + m
-        return remote(
-            second_ref(s, o, i, m), land2.at[s, o, i, m], rs_s.at[s, at], rs_r.at[s, at],
-            orders[o][3](dirs[i]),
-        )
-
     both = [(o, i) for o in range(2) for i in range(2)]
+    rel_y = [mod4(k - y) for k in range(SIDE)]
 
     def phase0(s):
-        for o in range(2):
-
-            def tile(t, carry):
-                rows = rows_all[pl.ds(t * SIDE, SIDE)].reshape(SIDE * ROWS, FEATS)
-                res = jnp.dot(rows, w_in[s, o], preferred_element_type=F32).astype(BF16)
-                res = res.reshape(SIDE, ROWS, WIDE)
-                if o == 0:
-                    part[s, 0, t] = res
-                else:
-                    part[s, 1, :, t] = res
-                return carry
-
-            lax.fori_loop(0, SIDE, tile, 0)
-            for i in range(2):
-                first_copy(s, o, i, 0).start()
-            for i in range(2):
-                first_copy(s, o, i, 1).start()
-
-    def add_into(ref, land):
-        ref[...] = (ref[...].astype(F32) + land[...].astype(F32)).astype(BF16)
+        def tile(t, carry):
+            rows = rows_all[pl.ds(t * SIDE, SIDE)].reshape(SIDE * ROWS, FEATS)
+            res = jnp.dot(rows, w_in[s], preferred_element_type=F32).astype(BF16)
+            rel_x = mod4(t - x)
+            for k in range(SIDE):
+                block = res[k * ROWS : (k + 1) * ROWS].reshape(2, HALF, 2 * WIDE)
+                part[s, 0, pl.ds((rel_x * SIDE + rel_y[k]) * 2, 2)] = block[:, :, :WIDE]
+                part[s, 1, pl.ds((rel_y[k] * SIDE + rel_x) * 2, 2)] = block[:, :, WIDE:]
+            return carry
+
+        lax.fori_loop(0, SIDE, tile, 0)
+        for o, i in both:
+            rs_copy(s, o, 0, i).start()
+
+    def add_into(ref, *lands):
+        res = ref[...].astype(F32)
+        for land in lands:
+            res += land[...].astype(F32)
+        ref[...] = res.astype(BF16)
 
     def phase1(s):
         for o, i in both:
-            first_copy(s, o, i, 0).wait()
-            add_into(first_ref(s, o, i, 2), land1.at[s, o, i, 0])
-            first_copy(s, o, i, 2).start()
+            rs_copy(s, o, 0, i).wait()
+            first, size = near1[i]
+            add_into(part.at[s, o, pl.ds(first, size)], land1.at[s, o, i, pl.ds(4 - 4 * i, 4)])
+            rs_copy(s, o, 1, i).start()
 
     def phase2(s):
         for o in range(2):
-            p1 = orders[o][0]
-            for i in range(2):
-                first_copy(s, o, i, 1).wait()
-                first_copy(s, o, i, 2).wait()
-            for i in range(2):
-                ref = part.at[s, o, p1, pl.ds(2 * i, 2)]
-                ref[...] = (
-                    ref[...].astype(F32)
-                    + land1[s, o, i, 2].astype(F32)
-                    + land1[s, o, 1 - i, 1].astype(F32)
-                ).astype(BF16)
-            for i in range(2):
-                second_copy(s, o, i, 0).start()
-                second_copy(s, o, i, 1).start()
+            for i in range(2):
+                rs_copy(s, o, 1, i).wait()
+            for i in range(2):
+                add_into(
+                    part.at[s, o, pl.ds(4 * i, 4)],
+                    last1.at[s, o, i],
+                    land1.at[s, o, 1 - i, pl.ds(4 - 4 * i, 4)],
+                )
+            for i in range(2):
+                rs_copy(s, o, 2, i).start()
 
     def phase3(s):
         for o, i in both:
-            second_copy(s, o, i, 0).wait()
-            add_into(second_ref(s, o, i, 2), land2.at[s, o, i, 0])
-            second_copy(s, o, i, 2).start()
+            rs_copy(s, o, 2, i).wait()
+            first, size = near2[i]
+            add_into(part.at[s, o, pl.ds(first, size)], land2.at[s, o, i, pl.ds(1 - i, 1)])
+            rs_copy(s, o, 3, i).start()
 
     def attend(left, right):
         seg_row = seg[...].astype(F32)
@@ -362,7 +351,7 @@
         allowed = (key_at <= row_at) & (seg_row == own)
         keys = kv_all[:, :, 0:HEAD].reshape(TOKENS, HEAD)
         vals = kv_all[:, :, HEAD : 2 * HEAD].reshape(TOKENS, HEAD)
-        cosine, sine = turn[0, 0], turn[0, 1]
+        cosine, sine = turn[0, 0] * HEAD**-0.5, turn[0, 1] * HEAD**-0.5
         groups = [v[:, k * 128 : (k + 1) * 128] for v in (left, right) for k in range(3)]
         pieces = []
         for h in range(3):
@@ -370,7 +359,7 @@
             query = jnp.concatenate([a * cosine - b * sine, a * sine + b * cosine], 1).astype(BF16)
             scores = lax.dot_general(
                 query, keys, (((1,), (1,)), ((), ())), preferred_element_type=F32
-            ) * (HEAD**-0.5)
+            )
             expos = jnp.where(allowed, jnp.exp(scores), 0.0)
             probs = (expos / jnp.sum(expos, 1, keepdims=True)).astype(BF16)
             res = jnp.dot(probs, vals, preferred_element_type=F32).astype(BF16)
@@ -378,36 +367,37 @@
         return jnp.concatenate(pieces[:3], 1), jnp.concatenate(pieces[3:], 1)
 
     def put(u, block):
-        mixed[u, 0, y, x] = block[0:HALF]
-        mixed[u, 1, x, y] = block[HALF:ROWS]
+        mixed[u, 0, 0, 0] = block[0:HALF]
+        mixed[u, 1, 0, 0] = block[HALF:ROWS]
 
     def gather_copy(u, o, k, i):
-        p1, p2, dev1, dev2 = orders[o]
         d = dirs[i]
+        away, near = (3, 1)[i], (3, 1)[i]
+        dev = devs[o][k // 2](d)
         if k == 0:
-            ref, dev = mixed.at[u, o, p2, p1], dev1(d)
+            src, dst = mixed.at[u, o, 0, 0], mixed.at[u, o, 0, away]
         elif k == 1:
-            ref, dev = mixed.at[u, o, p2, mod4(p1 - d), pl.ds(i * QUARTER, QUARTER)], dev1(d)
+            rows = pl.ds(i * QUARTER, QUARTER)
+            src, dst = mixed.at[u, o, 0, near, rows], mixed.at[u, o, 0, 2, rows]
         elif k == 2:
-            ref, dev = mixed.at[u, o, p2], dev2(d)
+            src, dst = mixed.at[u, o, 0], mixed.at[u, o, away]
         else:
-            ref, dev = mixed.at[u, o, mod4(p2 - d), pl.ds(2 * i, 2)], dev2(d)
+            cut = pl.ds(2 * i, 2)
+            src, dst = mixed.at[u, o, near, cut], mixed.at[u, o, 2, cut]
         at = o * 8 + k * 2 + i
-        return remote(ref, ref, ag_s.at[u, at], ag_r.at[u, at], dev)
+        return remote(src, dst, ag_s.at[u, at], ag_r.at[u, at], dev)
 
     def phase4(s):
         sums = []
         for o in range(2):
-            p1, p2 = orders[o][0], orders[o][1]
-            for i in range(2):
-                second_copy(s, o, i, 1).wait()
-                second_copy(s, o, i, 2).wait()
+            for i in range(2):
+                rs_copy(s, o, 3, i).wait()
             sums.append(
                 jnp.concatenate(
                     [
-                        part[s, o, p1, p2, i * HALF : (i + 1) * HALF].astype(F32)
-                        + land2[s, o, i, 2].astype(F32)
-                        + land2[s, o, 1 - i, 1].astype(F32)
+                        part[s, o, i].astype(F32)
+                        + last2[s, o, i, 0].astype(F32)
+                        + land2[s, o, 1 - i, 1 - i].astype(F32)
                         for i in range(2)
                     ],
                     0,
@@ -490,9 +480,9 @@
     offsets = (4, 3, -3, 2, -2, 1, -1, 0)
 
     def block_rows(block):
-        bx, by = block // SIDE, block % SIDE
+        bx, by = mod4(block // SIDE - x), mod4(block % SIDE - y)
         one = total[0, pl.ds(pl.multiple_of((by * SIDE + bx) * HALF, HALF), HALF)]
-        two = total[1, pl.ds(pl.multiple_of(block * HALF, HALF), HALF)]
+        two = total[1, pl.ds(pl.multiple_of((bx * SIDE + by) * HALF, HALF), HALF)]
         return jnp.concatenate([one, two], 0)
 
     def sib_sum(k):
@@ -551,7 +541,7 @@
     anywhere = pl.BlockSpec(memory_space=pl.ANY)
     dma = pltpu.SemaphoreType.DMA
     scratch = [
-        pltpu.VMEM((STEPS, 2, FEATS, WIDE), BF16),
+        pltpu.VMEM((STEPS, FEATS, 2 * WIDE), BF16),
         pltpu.VMEM((UNITS, WIDE, FEATS), BF16),
         pltpu.VMEM((FEATS, 512), BF16),
         pltpu.VMEM((2, 2, ROWS, 128), F32),
@@ -563,9 +553,11 @@
         pltpu.VMEM((ROWS, 128), BF16),
         pltpu.VMEM((4, ROWS, 128), BF16),
         pltpu.VMEM((GROUP, ROWS, 512), BF16),
-        pltpu.VMEM((STEPS, 2, SIDE, SIDE, ROWS, WIDE), BF16),
-        pltpu.VMEM((STEPS, 2, 2, 3, 2, ROWS, WIDE), BF16),
-        pltpu.VMEM((STEPS, 2, 2, 3, HALF, WIDE), BF16),
+        pltpu.VMEM((STEPS, 2, 2 * GROUP, HALF, WIDE), BF16),
+        pltpu.VMEM((STEPS, 2, 2, 8, HALF, WIDE), BF16),
+        pltpu.VMEM((STEPS, 2, 2, 4, HALF, WIDE), BF16),
+        pltpu.VMEM((STEPS, 2, 2, 2, HALF, WIDE), BF16),
+        pltpu.VMEM((STEPS, 2, 2, 1, HALF, WIDE), BF16),
         pltpu.VMEM((UNITS, 2, SIDE, SIDE, HALF, WIDE), BF16),
         pltpu.VMEM((2, GROUP * HALF, FEATS), F32),
         pltpu.VMEM((RING, ROWS, FEATS), BF16),
@@ -582,8 +574,8 @@
         dma((8, 2)),
         dma((8, 2)),
         dma((8, 2)),
-        dma((STEPS, 24)),
-        dma((STEPS, 24)),
+        dma((STEPS, 16)),
+        dma((STEPS, 16)),
         dma((UNITS, 16)),
         dma((UNITS, 16)),
         dma((16,)),
@@ -600,7 +592,7 @@
         ),
     )(
         activations,
-        ln_gain.reshape(1, FEATS),
+        ln_gain,
         segments.reshape(1, TOKENS),
         jnp.asarray(tables()),
         w_query,

time: 155 us -> 151 us (0.974)
  Pallas kernels: 152 us -> 150 us
    pallas_call x1, Pallas kernels: 152 us -> 150 us  [per_device(): pl.pallas_call(block_kernel, out_shape=jax.ShapeDtypeStruct((ROWS, FEATS)...]
where the time goes in v2:
time: 151 us
  Pallas kernels  150 us (99%)
  local copies, waits for them, and re-layouts  1.53 us (1%)
    pallas_call x1, Pallas kernels, per_device(): pl.pallas_call(block_kernel, out_shape=jax.ShapeDtypeStruct((ROWS, FEATS)...  150 us

profile of v2, /device:TPU:32, one launch (start us, length us, event | category | flops | bytes accessed | tf_op | source)
XLA Modules:
  0.0 151.0 jit_solution(3205710019740669761)
XLA Ops:
  0.0 149.5 %shard_map.100 = bf16[64,640]{1,0:T(8,128)(2,1)} custom-call(bf16[64,640]{1,0:T(8,128)(2,1)} %act.1, f32[640]{0:T(1024)} %gain.1, s32[1,1024]{1,0:T(1,128)} %bitcast.1, f32[2,1024,128]{2,1,0:T(8,128)} %constant.2.clone.table, bf16[640,768]{1,0:T(8,128)(2,1)} %w_query.1, bf16[640,512]{1,0:T(8,128)(2,1)} %w_pairs.1, bf16[640,2304]{1,0:T(8,128)(2,1)} %w_gate.1, ...), custom_call_target="tpu_custom_call" | custom-call | tf_op jit(solution)/shard_map/pallas_call | solution.py:584
  149.5 1.5 %copy.12 = bf16[64,640]{1,0:T(8,128)(2,1)} copy(bf16[64,640]{1,0:T(8,128)(2,1)} %shard_map.100) | data formatting | bytes 163840

commit v3 on v2

--- a/solution.py
+++ b/solution.py
@@ -20,6 +20,7 @@
 STEPS = 7
 UNITS = 8
 HALF = ROWS // 2
+QUARTERS = 4
 QUARTER = ROWS // 4
 F32 = jnp.float32
 BF16 = jnp.bfloat16
@@ -51,6 +52,8 @@
     turn,
     stat,
     stat_in,
+    stat_all,
+    raw_all,
     rows_all,
     pair_part,
     pair_in,
@@ -60,6 +63,7 @@
     part,
     land1,
     last1,
+    half_sum,
     land2,
     last2,
     mixed,
@@ -67,7 +71,6 @@
     sib_out,
     sib_in,
     ring_out,
-    ring_half,
     ring_in,
     w_sem,
     wb_sem,
@@ -76,6 +79,10 @@
     small_r,
     zx_s,
     zx_r,
+    zt_s,
+    zt_r,
+    rq_s,
+    rq_r,
     zk_s,
     zk_r,
     rs_s,
@@ -143,17 +150,30 @@
             src = w_down.at[pl.ds((u - 2) * WIDE, WIDE)]
         return pltpu.make_async_copy(src, w_back.at[u], wb_sem.at[u])
 
-    def turn_copy(k, i):
-        first = (hid if k == 0 else ffn) * ROWS
-        return pltpu.make_async_copy(
-            table.at[i, pl.ds(first, ROWS)], turn.at[k, i], m_sem.at[1 + 2 * k + i]
-        )
+    def turn_copies(i):
+        copies = [
+            pltpu.make_async_copy(
+                table.at[i, pl.ds(pl.multiple_of(ffn * ROWS, ROWS), ROWS)],
+                turn.at[1, i],
+                m_sem.at[1 + 5 * i],
+            )
+        ]
+        for g in range(QUARTERS):
+            first = pl.multiple_of(g * (TOKENS // QUARTERS) + hid * QUARTER, QUARTER)
+            copies.append(
+                pltpu.make_async_copy(
+                    table.at[i, pl.ds(first, QUARTER)],
+                    turn.at[0, i, pl.ds(g * QUARTER, QUARTER)],
+                    m_sem.at[2 + 5 * i + g],
+                )
+            )
+        return copies
 
     kv_copy = pltpu.make_async_copy(w_pairs, w_kv, m_sem.at[0])
     kv_copy.start()
-    for k in range(2):
-        for i in range(2):
-            turn_copy(k, i).start()
+    for i in range(2):
+        for copy in turn_copies(i):
+            copy.start()
     for s in range(STEPS):
         for o in range(2):
             w_copy(s, o).start()
@@ -208,39 +228,124 @@
             for i in range(2):
                 z_copy(buf, sems, j, i).wait()
             sib_copy(buf, sems, 4).start()
-            for off in (0, 1, -1, 2, -2, 3, -3, 4):
-                sib_copy(buf, sems, off).wait()
-
+
+    def sib_wait(buf, sems, *offs):
+        for off in offs:
+            sib_copy(buf, sems, off).wait()
+
+    def stat_z(j, i):
+        ref = stat_all.at[mod8(z - (j - 1) * dirs[i])]
+        return remote(ref, ref, zt_s.at[j, i], zt_r.at[j, i], dev_z(dirs[i]))
+
+    def stat_step(j):
+        for i in range(2):
+            if (j, i) == (4, 1):
+                continue
+            stat_z(j, i).wait()
+            if j < 3 + (i == 0):
+                stat_z(j + 1, i).start()
+
+    def quarter_copy(j, g, o, i):
+        at = o * 2 + i
+        return remote(
+            part.at[0, o, g, pl.ds((6, 10)[i], 4)],
+            land1.at[0, o, i, g],
+            rq_s.at[j, at],
+            rq_r.at[j, at],
+            devs[o][0](dirs[i]),
+        )
+
+    both = [(o, i) for o in range(2) for i in range(2)]
+    rel_x = [mod4(k - x) for k in range(SIDE)]
+    rel_y = [mod4(k - y) for k in range(SIDE)]
+    places = (
+        [rel_x[h // SIDE] * SIDE + rel_y[h % SIDE] for h in range(GROUP)],
+        [rel_y[h % SIDE] * SIDE + rel_x[h // SIDE] for h in range(GROUP)],
+    )
+
+    def products(s, g):
+        rows = rows_all[pl.ds(g * QUARTERS, QUARTERS)].reshape(QUARTERS * ROWS, FEATS)
+        res = jnp.dot(rows, w_in[s], preferred_element_type=F32).astype(BF16)
+        for h in range(GROUP):
+            block = res[h * QUARTER : (h + 1) * QUARTER]
+            for o in range(2):
+                part[s, o, g, places[o][h]] = block[:, o * WIDE : (o + 1) * WIDE]
+
+    eye = lax.broadcasted_iota(jnp.int32, (ROWS, 128), 0) == lax.broadcasted_iota(
+        jnp.int32, (ROWS, 128), 1
+    )
+    line = lax.broadcasted_iota(jnp.int32, (8, 128), 0)
+
+    def to_row(column):
+        return jnp.sum(jnp.where(eye, column, 0.0), 0, keepdims=True)
+
+    def to_column(row):
+        return jnp.sum(jnp.where(eye, row, 0.0), 1, keepdims=True)
+
+    def norm(rows, tile):
+        mean, scale = to_column(tile[0:1]), to_column(tile[1:2])
+        return ((rows.astype(F32) - mean) * scale * gain[...].reshape(1, FEATS)).astype(BF16)
+
+    zx = (zx_s, zx_r)
+    zk = (zk_s, zk_r)
+    raw_all[ffn] = act[...]
+    z_start(raw_all, zx)
     values = act[...].astype(F32)
     mean = jnp.mean(values, 1, keepdims=True)
     square = jnp.sum((values - mean) ** 2, 1, keepdims=True)
-    lane = lax.broadcasted_iota(jnp.int32, (ROWS, 128), 1)
+    mean, square = to_row(mean), to_row(square)
     for a, count in ((0, FEATS), (1, FEATS * SIDE)):
-        stat[a] = jnp.where(lane < 64, mean, square)
+        stat[a] = jnp.where(line == 0, mean, square)
         each(stat_copy, a, "start")
         if a == 0:
             total[...] = jnp.zeros_like(total)
+        else:
+            z_step(raw_all, zx, 1)
         each(stat_copy, a, "wait")
-        means = [mean] + [stat_in[a, d, :, 0:1] for d in range(3)]
-        squares = [square] + [stat_in[a, d, :, 64:65] for d in range(3)]
+        means = [mean] + [stat_in[a, d, 0:1] for d in range(3)]
+        squares = [square] + [stat_in[a, d, 1:2] for d in range(3)]
         mean = (means[0] + means[1] + means[2] + means[3]) * 0.25
         square = squares[0] + squares[1] + squares[2] + squares[3]
         for one in means:
             square += count * (one - mean) ** 2
     scale = lax.rsqrt(square * (1.0 / D) + EPSILON)
-    values = act[...].astype(F32)
-    normed = ((values - mean) * scale * gain[...].reshape(1, FEATS)).astype(BF16)
-    rows_all[ffn] = normed
-    zx = (zx_s, zx_r)
-    zk = (zk_s, zk_r)
-    z_start(rows_all, zx)
-
+    stat_all[z, core] = jnp.where(line == 0, mean, scale)
+    stat_sib = remote(
+        stat_all.at[z, core], stat_all.at[z, core], zt_s.at[0, 0], zt_r.at[0, 0], sibling
+    )
+    stat_sib.start()
+    normed = norm(act[...], stat_all[z, core])
+    stat_sib.wait()
+    for i in range(2):
+        stat_z(1, i).start()
     kv_copy.wait()
     pairs = jnp.dot(normed, w_kv[...], preferred_element_type=F32).astype(BF16)
     for q in range(4):
         pair_part[q] = pairs[:, q * 128 : (q + 1) * 128]
     each(pair_copy, 0, "start")
-    z_step(rows_all, zx, 1)
+    for o in range(2):
+        w_copy(0, o).wait()
+
+    pair = z // 2
+    turned = 1 - 2 * (z % 2)
+    order = (pair, mod4(pair - turned), mod4(pair + turned), mod4(pair + 2))
+
+    def first_products(j):
+        g = order[j]
+
+        def one(k, carry):
+            rows_all[g * 4 + k] = norm(raw_all[g * 4 + k], stat_all[g * 2 + k // 2, k % 2])
+            return carry
+
+        lax.fori_loop(0, QUARTERS, one, 0)
+        products(0, g)
+        for o, i in both:
+            quarter_copy(j, g, o, i).start()
+
+    z_step(raw_all, zx, 2)
+    stat_step(1)
+    sib_wait(raw_all, zx, 0, 1, -1)
+    first_products(0)
     each(pair_copy, 0, "wait")
     pair_sum[...] = (
         pair_part[x].astype(F32)
@@ -249,7 +354,10 @@
         + pair_in[0, 2].astype(F32)
     ).astype(BF16)
     each(pair_copy, 1, "start")
-    z_step(rows_all, zx, 2)
+    z_step(raw_all, zx, 3)
+    stat_step(2)
+    sib_wait(raw_all, zx, 2, -2)
+    first_products(1)
     each(pair_copy, 1, "wait")
     pair_all[x] = (
         pair_sum[...].astype(F32)
@@ -258,69 +366,82 @@
         + pair_in[1, 2].astype(F32)
     ).astype(BF16)
     each(pair_copy, 2, "start")
-    z_step(rows_all, zx, 3)
+    z_step(raw_all, zx, 4)
+    stat_step(3)
+    sib_wait(raw_all, zx, 3, -3)
+    first_products(2)
+    stat_step(4)
+    sib_wait(raw_all, zx, 4)
+    first_products(3)
     each(pair_copy, 2, "wait")
-    for k in range(2):
-        for i in range(2):
-            turn_copy(k, i).wait()
+    for i in range(2):
+        for copy in turn_copies(i):
+            copy.wait()
     first, second = pair_all[0].astype(F32), pair_all[1].astype(F32)
     kv_all[ffn, :, 0:128] = (first * turn[1, 0] - second * turn[1, 1]).astype(BF16)
     kv_all[ffn, :, 128:256] = (first * turn[1, 1] + second * turn[1, 0]).astype(BF16)
     kv_all[ffn, :, 256:384] = pair_all[2]
     kv_all[ffn, :, 384:512] = pair_all[3]
-    z_step(rows_all, zx, 4)
-
-    for s in range(STEPS):
+    z_start(kv_all, zk)
+
+    for s in range(1, STEPS):
         for o in range(2):
             w_copy(s, o).wait()
     for u in range(UNITS):
         wb_copy(u).wait()
 
-    far1 = ((12, 8), (20, 8))
-    near1 = ((8, 4), (28, 4))
+    far1 = ((6, 4), (10, 4))
+    near1 = ((4, 2), (14, 2))
     far2 = ((3, 2), (5, 2))
     near2 = ((2, 1), (7, 1))
 
     def rs_copy(s, o, k, i):
         first, size = (far1, near1, far2, near2)[k][i]
         at = o * 8 + k * 2 + i
+        if k < 2:
+            src = part.at[s, o, :, pl.ds(first, size)]
+        else:
+            src = half_sum.at[s, o, pl.ds(first, size)]
         return remote(
-            part.at[s, o, pl.ds(first, size)],
+            src,
             (land1, last1, land2, last2)[k].at[s, o, i],
             rs_s.at[s, at],
             rs_r.at[s, at],
             devs[o][k // 2](dirs[i]),
         )
 
-    both = [(o, i) for o in range(2) for i in range(2)]
-    rel_y = [mod4(k - y) for k in range(SIDE)]
-
     def phase0(s):
-        def tile(t, carry):
-            rows = rows_all[pl.ds(t * SIDE, SIDE)].reshape(SIDE * ROWS, FEATS)
-            res = jnp.dot(rows, w_in[s], preferred_element_type=F32).astype(BF16)
-            rel_x = mod4(t - x)
-            for k in range(SIDE):
-                block = res[k * ROWS : (k + 1) * ROWS].reshape(2, HALF, 2 * WIDE)
-                part[s, 0, pl.ds((rel_x * SIDE + rel_y[k]) * 2, 2)] = block[:, :, :WIDE]
-                part[s, 1, pl.ds((rel_y[k] * SIDE + rel_x) * 2, 2)] = block[:, :, WIDE:]
+        def tile(g, carry):
+            products(s, g)
             return carry
 
-        lax.fori_loop(0, SIDE, tile, 0)
+        lax.fori_loop(0, QUARTERS, tile, 0)
         for o, i in both:
             rs_copy(s, o, 0, i).start()
 
-    def add_into(ref, *lands):
-        res = ref[...].astype(F32)
-        for land in lands:
-            res += land[...].astype(F32)
-        ref[...] = res.astype(BF16)
+    def added(first, *rest):
+        res = first.astype(F32)
+        for one in rest:
+            res += one.astype(F32)
+        return res
 
     def phase1(s):
+        @pl.when(s == 0)
+        def _():
+            for j in range(QUARTERS):
+                for o, i in both:
+                    quarter_copy(j, order[j], o, i).wait()
+
+        @pl.when(s > 0)
+        def _():
+            for o, i in both:
+                rs_copy(s, o, 0, i).wait()
+
         for o, i in both:
-            rs_copy(s, o, 0, i).wait()
             first, size = near1[i]
-            add_into(part.at[s, o, pl.ds(first, size)], land1.at[s, o, i, pl.ds(4 - 4 * i, 4)])
+            part[s, o, :, first : first + size] = added(
+                part[s, o, :, first : first + size], land1[s, o, i, :, 2 - 2 * i : 4 - 2 * i]
+            ).astype(BF16)
             rs_copy(s, o, 1, i).start()
 
     def phase2(s):
@@ -328,25 +449,32 @@
             for i in range(2):
                 rs_copy(s, o, 1, i).wait()
             for i in range(2):
-                add_into(
-                    part.at[s, o, pl.ds(4 * i, 4)],
-                    last1.at[s, o, i],
-                    land1.at[s, o, 1 - i, pl.ds(4 - 4 * i, 4)],
-                )
+                cut = slice(2 - 2 * i, 4 - 2 * i)
+                res = added(
+                    part[s, o, :, 2 * i : 2 * i + 2],
+                    last1[s, o, i],
+                    land1[s, o, 1 - i, :, cut],
+                ).astype(BF16)
+                for b in range(2):
+                    for r in range(2):
+                        half_sum[s, o, (2 * i + b) * 2 + r] = res[2 * r : 2 * r + 2, b].reshape(
+                            HALF, WIDE
+                        )
             for i in range(2):
                 rs_copy(s, o, 2, i).start()
 
     def phase3(s):
         for o, i in both:
             rs_copy(s, o, 2, i).wait()
-            first, size = near2[i]
-            add_into(part.at[s, o, pl.ds(first, size)], land2.at[s, o, i, pl.ds(1 - i, 1)])
+            first = near2[i][0]
+            half_sum[s, o, first] = added(half_sum[s, o, first], land2[s, o, i, 1 - i]).astype(BF16)
             rs_copy(s, o, 3, i).start()
 
     def attend(left, right):
         seg_row = seg[...].astype(F32)
         key_at = lax.broadcasted_iota(jnp.int32, (ROWS, TOKENS), 1)
-        row_at = lax.broadcasted_iota(jnp.int32, (ROWS, TOKENS), 0) + hid * ROWS
+        row_at = lax.broadcasted_iota(jnp.int32, (ROWS, TOKENS), 0)
+        row_at = row_at + (TOKENS // QUARTERS - QUARTER) * (row_at // QUARTER) + hid * QUARTER
         own = jnp.sum(jnp.where(key_at == row_at, seg_row, 0.0), 1, keepdims=True)
         allowed = (key_at <= row_at) & (seg_row == own)
         keys = kv_all[:, :, 0:HEAD].reshape(TOKENS, HEAD)
@@ -395,7 +523,7 @@
             sums.append(
                 jnp.concatenate(
                     [
-                        part[s, o, i].astype(F32)
+                        half_sum[s, o, i].astype(F32)
                         + last2[s, o, i, 0].astype(F32)
                         + land2[s, o, 1 - i, 1 - i].astype(F32)
                         for i in range(2)
@@ -448,16 +576,18 @@
                 )
 
     def slot(t, carry):
-        for k, fn in enumerate((phase0, phase1, phase2, phase3)):
+        pl.when(t < STEPS)(lambda: phase0(t))
+        for k, fn in ((1, phase1), (2, phase2), (3, phase3)):
             s = t - k
             pl.when((s >= 0) & (s < STEPS))(lambda fn=fn, s=s: fn(s))
 
-        @pl.when(t == 0)
-        def _():
-            z_start(kv_all, zk)
-
         for j in range(1, 5):
-            pl.when(t == j)(lambda j=j: z_step(kv_all, zk, j))
+
+            @pl.when(t == j)
+            def _(j=j):
+                z_step(kv_all, zk, j)
+                if j == 4:
+                    sib_wait(kv_all, zk, 0, 1, -1, 2, -2, 3, -3, 4)
 
         s4 = t - 4
         pl.when((s4 >= 0) & (s4 < STEPS))(lambda: phase4(s4))
@@ -475,15 +605,20 @@
 
         return carry
 
-    lax.fori_loop(0, STEPS + 8, slot, 0)
+    lax.fori_loop(1, STEPS + 8, slot, 0)
 
     offsets = (4, 3, -3, 2, -2, 1, -1, 0)
 
-    def block_rows(block):
-        bx, by = mod4(block // SIDE - x), mod4(block % SIDE - y)
-        one = total[0, pl.ds(pl.multiple_of((by * SIDE + bx) * HALF, HALF), HALF)]
-        two = total[1, pl.ds(pl.multiple_of((bx * SIDE + by) * HALF, HALF), HALF)]
-        return jnp.concatenate([one, two], 0)
+    def half_rows(block, h):
+        g = block // SIDE
+        o = g // 2
+        px = mod4(block % SIDE - x)
+        pieces = []
+        for k in (2 * h, 2 * h + 1):
+            place = jnp.where(o == 0, rel_y[k] * SIDE + px, px * SIDE + rel_y[k])
+            first = pl.multiple_of(place * HALF + (g % 2) * QUARTER, QUARTER)
+            pieces.append(total[o, pl.ds(first, QUARTER)])
+        return jnp.concatenate(pieces, 0)
 
     def sib_sum(k):
         at = mod8(z + offsets[k])
@@ -491,49 +626,43 @@
 
     for k in range(RING):
         at = mod8(z + offsets[k])
-        sib_out[at] = block_rows(at * 2 + 1 - core).astype(BF16)
+        for h in range(2):
+            sib_out[at, h * HALF : (h + 1) * HALF] = half_rows(at * 2 + 1 - core, h).astype(BF16)
         sib_sum(k).start()
 
-    def chip_sum(k):
+    def chip_sum(k, h):
         at = mod8(z + offsets[k])
-        sib_sum(k).wait()
-        return block_rows(at * 2 + core) + sib_in[at].astype(F32)
-
-    def half_copy(i):
+        return half_rows(at * 2 + core, h) + sib_in[at, h * HALF : (h + 1) * HALF].astype(F32)
+
+    def ring_copy(j, i, h):
+        at = 8 + j * 4 + i * 2 + h
         return remote(
-            ring_out.at[0, i, pl.ds(0, HALF)], ring_half.at[i], zr_s.at[8 + i], zr_r.at[8 + i],
-            dev_z(dirs[i]),
+            ring_out.at[j, i, h], ring_in.at[j, i, h], zr_s.at[at], zr_r.at[at], dev_z(dirs[i])
         )
 
-    def full_copy(j, i):
-        at = 10 + 2 * j + i
-        return remote(
-            ring_out.at[1 + j, i], ring_in.at[j, i], zr_s.at[at], zr_r.at[at], dev_z(dirs[i])
-        )
-
-    far = chip_sum(0)
+    sib_sum(0).wait()
     for i in range(2):
-        ring_out[0, i, 0:HALF] = far[i * HALF : (i + 1) * HALF].astype(BF16)
-        half_copy(i).start()
-    for i in range(2):
-        here = chip_sum(1 + i)
-        half_copy(i).wait()
-        come = ring_half[i].astype(F32)
-        pad = jnp.zeros((HALF, FEATS), F32)
-        come = jnp.concatenate([come, pad] if i == 0 else [pad, come], 0)
-        ring_out[1, i] = (here + come).astype(BF16)
-        full_copy(0, i).start()
-    for j in (1, 2):
+        ring_out[0, i, i] = chip_sum(0, i).astype(BF16)
+        ring_copy(0, i, i).start()
+    for j in (1, 2, 3):
         for i in range(2):
-            here = chip_sum(1 + 2 * j + i)
-            full_copy(j - 1, i).wait()
-            ring_out[1 + j, i] = (here + ring_in[j - 1, i].astype(F32)).astype(BF16)
-            full_copy(j, i).start()
-    here = chip_sum(7) + act[...].astype(F32)
-    for i in range(2):
-        full_copy(2, i).wait()
-        here += ring_in[2, i].astype(F32)
-    out[...] = here.astype(BF16)
+            sib_sum(2 * j - 1 + i).wait()
+        for turn_of in range(2):
+            for i in range(2):
+                h = (1 - i, i)[turn_of]
+                here = chip_sum(2 * j - 1 + i, h)
+                if j > 1 or h == i:
+                    ring_copy(j - 1, i, h).wait()
+                    here += ring_in[j - 1, i, h].astype(F32)
+                ring_out[j, i, h] = here.astype(BF16)
+                ring_copy(j, i, h).start()
+    sib_sum(7).wait()
+    for h in range(2):
+        here = chip_sum(7, h) + act[h * HALF : (h + 1) * HALF].astype(F32)
+        for i in range(2):
+            ring_copy(3, i, h).wait()
+            here += ring_in[3, i, h].astype(F32)
+        out[h * HALF : (h + 1) * HALF] = here.astype(BF16)
 
 
 def per_device(activations, ln_gain, segments, w_query, w_key_value, w_gate, w_up, w_out, w_down):
@@ -545,41 +674,47 @@
         pltpu.VMEM((UNITS, WIDE, FEATS), BF16),
         pltpu.VMEM((FEATS, 512), BF16),
         pltpu.VMEM((2, 2, ROWS, 128), F32),
-        pltpu.VMEM((2, ROWS, 128), F32),
-        pltpu.VMEM((2, 3, ROWS, 128), F32),
+        pltpu.VMEM((2, 8, 128), F32),
+        pltpu.VMEM((2, 3, 8, 128), F32),
+        pltpu.VMEM((RING, 2, 8, 128), F32),
+        pltpu.VMEM((GROUP, ROWS, FEATS), BF16),
         pltpu.VMEM((GROUP, ROWS, FEATS), BF16),
         pltpu.VMEM((4, ROWS, 128), BF16),
         pltpu.VMEM((2, 3, ROWS, 128), BF16),
         pltpu.VMEM((ROWS, 128), BF16),
         pltpu.VMEM((4, ROWS, 128), BF16),
         pltpu.VMEM((GROUP, ROWS, 512), BF16),
-        pltpu.VMEM((STEPS, 2, 2 * GROUP, HALF, WIDE), BF16),
-        pltpu.VMEM((STEPS, 2, 2, 8, HALF, WIDE), BF16),
-        pltpu.VMEM((STEPS, 2, 2, 4, HALF, WIDE), BF16),
+        pltpu.VMEM((STEPS, 2, QUARTERS, GROUP, QUARTER, WIDE), BF16),
+        pltpu.VMEM((STEPS, 2, 2, QUARTERS, 4, QUARTER, WIDE), BF16),
+        pltpu.VMEM((STEPS, 2, 2, QUARTERS, 2, QUARTER, WIDE), BF16),
+        pltpu.VMEM((STEPS, 2, 2 * SIDE, HALF, WIDE), BF16),
         pltpu.VMEM((STEPS, 2, 2, 2, HALF, WIDE), BF16),
         pltpu.VMEM((STEPS, 2, 2, 1, HALF, WIDE), BF16),
         pltpu.VMEM((UNITS, 2, SIDE, SIDE, HALF, WIDE), BF16),
         pltpu.VMEM((2, GROUP * HALF, FEATS), F32),
         pltpu.VMEM((RING, ROWS, FEATS), BF16),
         pltpu.VMEM((RING, ROWS, FEATS), BF16),
-        pltpu.VMEM((4, 2, ROWS, FEATS), BF16),
-        pltpu.VMEM((2, HALF, FEATS), BF16),
-        pltpu.VMEM((3, 2, ROWS, FEATS), BF16),
+        pltpu.VMEM((4, 2, 2, HALF, FEATS), BF16),
+        pltpu.VMEM((4, 2, 2, HALF, FEATS), BF16),
         dma((STEPS, 2)),
         dma((UNITS,)),
-        dma((5,)),
+        dma((11,)),
         dma((5, 3)),
         dma((5, 3)),
         dma((8, 2)),
         dma((8, 2)),
+        dma((5, 2)),
+        dma((5, 2)),
+        dma((QUARTERS, 4)),
+        dma((QUARTERS, 4)),
         dma((8, 2)),
         dma((8, 2)),
         dma((STEPS, 16)),
         dma((STEPS, 16)),
         dma((UNITS, 16)),
         dma((UNITS, 16)),
-        dma((16,)),
-        dma((16,)),
+        dma((24,)),
+        dma((24,)),
     ]
     return pl.pallas_call(
         block_kernel,

time: 151 us -> 141 us (0.934)
  Pallas kernels: 150 us -> 139 us
    pallas_call x1, Pallas kernels: 150 us -> 139 us  [per_device(): pl.pallas_call(block_kernel, out_shape=jax.ShapeDtypeStruct((ROWS, FEATS)...]
where the time goes in v3:
time: 141 us
  Pallas kernels  139 us (99%)
  local copies, waits for them, and re-layouts  1.53 us (1%)
    pallas_call x1, Pallas kernels, per_device(): pl.pallas_call(block_kernel, out_shape=jax.ShapeDtypeStruct((ROWS, FEATS)...  139 us

profile of v3, /device:TPU:32, one launch (start us, length us, event | category | flops | bytes accessed | tf_op | source)
XLA Modules:
  0.0 140.9 jit_solution(2868427584457941184)
XLA Ops:
  0.0 139.3 %shard_map.100 = bf16[64,640]{1,0:T(8,128)(2,1)} custom-call(bf16[64,640]{1,0:T(8,128)(2,1)} %act.1, f32[640]{0:T(1024)} %gain.1, s32[1,1024]{1,0:T(1,128)} %bitcast.1, f32[2,1024,128]{2,1,0:T(8,128)} %constant.2.clone.table, bf16[640,768]{1,0:T(8,128)(2,1)} %w_query.1, bf16[640,512]{1,0:T(8,128)(2,1)} %w_pairs.1, bf16[640,2304]{1,0:T(8,128)(2,1)} %w_gate.1, ...), custom_call_target="tpu_custom_call" | custom-call | tf_op jit(solution)/shard_map/pallas_call | solution.py:719
  139.3 1.5 %copy.12 = bf16[64,640]{1,0:T(8,128)(2,1)} copy(bf16[64,640]{1,0:T(8,128)(2,1)} %shard_map.100) | data formatting | bytes 163840

commit v4 on v3

--- a/solution.py
+++ b/solution.py
@@ -18,6 +18,7 @@
 FEATS = D // GROUP
 WIDE = 384
 STEPS = 7
+EARLY = 2
 UNITS = 8
 HALF = ROWS // 2
 QUARTERS = 4
@@ -170,15 +171,6 @@
         return copies
 
     kv_copy = pltpu.make_async_copy(w_pairs, w_kv, m_sem.at[0])
-    kv_copy.start()
-    for i in range(2):
-        for copy in turn_copies(i):
-            copy.start()
-    for s in range(STEPS):
-        for o in range(2):
-            w_copy(s, o).start()
-    for u in range(UNITS):
-        wb_copy(u).start()
 
     pl.semaphore_wait(barrier, len(partners))
 
@@ -245,13 +237,13 @@
             if j < 3 + (i == 0):
                 stat_z(j + 1, i).start()
 
-    def quarter_copy(j, g, o, i):
+    def quarter_copy(s, j, g, o, i):
         at = o * 2 + i
         return remote(
-            part.at[0, o, g, pl.ds((6, 10)[i], 4)],
-            land1.at[0, o, i, g],
-            rq_s.at[j, at],
-            rq_r.at[j, at],
+            part.at[s, o, g, pl.ds((6, 10)[i], 4)],
+            land1.at[s, o, i, g],
+            rq_s.at[s * QUARTERS + j, at],
+            rq_r.at[s * QUARTERS + j, at],
             devs[o][0](dirs[i]),
         )
 
@@ -298,8 +290,15 @@
         stat[a] = jnp.where(line == 0, mean, square)
         each(stat_copy, a, "start")
         if a == 0:
+            kv_copy.start()
+            for s in range(EARLY):
+                for o in range(2):
+                    w_copy(s, o).start()
             total[...] = jnp.zeros_like(total)
         else:
+            for s in range(EARLY, STEPS):
+                for o in range(2):
+                    w_copy(s, o).start()
             z_step(raw_all, zx, 1)
         each(stat_copy, a, "wait")
         means = [mean] + [stat_in[a, d, 0:1] for d in range(3)]
@@ -323,8 +322,14 @@
     for q in range(4):
         pair_part[q] = pairs[:, q * 128 : (q + 1) * 128]
     each(pair_copy, 0, "start")
-    for o in range(2):
-        w_copy(0, o).wait()
+    for i in range(2):
+        for copy in turn_copies(i):
+            copy.start()
+    for u in range(UNITS):
+        wb_copy(u).start()
+    for s in range(EARLY):
+        for o in range(2):
+            w_copy(s, o).wait()
 
     pair = z // 2
     turned = 1 - 2 * (z % 2)
@@ -338,9 +343,10 @@
             return carry
 
         lax.fori_loop(0, QUARTERS, one, 0)
-        products(0, g)
-        for o, i in both:
-            quarter_copy(j, g, o, i).start()
+        for s in range(EARLY):
+            products(s, g)
+            for o, i in both:
+                quarter_copy(s, j, g, o, i).start()
 
     z_step(raw_all, zx, 2)
     stat_step(1)
@@ -384,7 +390,7 @@
     kv_all[ffn, :, 384:512] = pair_all[3]
     z_start(kv_all, zk)
 
-    for s in range(1, STEPS):
+    for s in range(EARLY, STEPS):
         for o in range(2):
             w_copy(s, o).wait()
     for u in range(UNITS):
@@ -426,13 +432,13 @@
         return res
 
     def phase1(s):
-        @pl.when(s == 0)
+        @pl.when(s < EARLY)
         def _():
             for j in range(QUARTERS):
                 for o, i in both:
-                    quarter_copy(j, order[j], o, i).wait()
-
-        @pl.when(s > 0)
+                    quarter_copy(s, j, order[j], o, i).wait()
+
+        @pl.when(s >= EARLY)
         def _():
             for o, i in both:
                 rs_copy(s, o, 0, i).wait()
@@ -481,17 +487,26 @@
         vals = kv_all[:, :, HEAD : 2 * HEAD].reshape(TOKENS, HEAD)
         cosine, sine = turn[0, 0] * HEAD**-0.5, turn[0, 1] * HEAD**-0.5
         groups = [v[:, k * 128 : (k + 1) * 128] for v in (left, right) for k in range(3)]
-        pieces = []
+        query = []
         for h in range(3):
             a, b = groups[2 * h], groups[2 * h + 1]
-            query = jnp.concatenate([a * cosine - b * sine, a * sine + b * cosine], 1).astype(BF16)
-            scores = lax.dot_general(
-                query, keys, (((1,), (1,)), ((), ())), preferred_element_type=F32
-            )
-            expos = jnp.where(allowed, jnp.exp(scores), 0.0)
-            probs = (expos / jnp.sum(expos, 1, keepdims=True)).astype(BF16)
-            res = jnp.dot(probs, vals, preferred_element_type=F32).astype(BF16)
-            pieces += [res[:, 0:128], res[:, 128:256]]
+            query.append(jnp.concatenate([a * cosine - b * sine, a * sine + b * cosine], 1))
+        scores = lax.dot_general(
+            jnp.concatenate(query, 0).astype(BF16),
+            keys,
+            (((1,), (1,)), ((), ())),
+            preferred_element_type=F32,
+        )
+        probs = []
+        for h in range(3):
+            expos = jnp.where(allowed, jnp.exp(scores[h * ROWS : (h + 1) * ROWS]), 0.0)
+            probs.append((expos / jnp.sum(expos, 1, keepdims=True)).astype(BF16))
+        res = jnp.dot(jnp.concatenate(probs, 0), vals, preferred_element_type=F32).astype(BF16)
+        pieces = [
+            res[h * ROWS : (h + 1) * ROWS, k * 128 : (k + 1) * 128]
+            for h in range(3)
+            for k in range(2)
+        ]
         return jnp.concatenate(pieces[:3], 1), jnp.concatenate(pieces[3:], 1)
 
     def put(u, block):
@@ -576,8 +591,8 @@
                 )
 
     def slot(t, carry):
-        pl.when(t < STEPS)(lambda: phase0(t))
-        for k, fn in ((1, phase1), (2, phase2), (3, phase3)):
+        pl.when((t >= EARLY) & (t < STEPS))(lambda: phase0(t))
+        for k, fn in ((1, phase1), (3, phase2), (4, phase3)):
             s = t - k
             pl.when((s >= 0) & (s < STEPS))(lambda fn=fn, s=s: fn(s))
 
@@ -589,10 +604,10 @@
                 if j == 4:
                     sib_wait(kv_all, zk, 0, 1, -1, 2, -2, 3, -3, 4)
 
-        s4 = t - 4
+        s4 = t - 5
         pl.when((s4 >= 0) & (s4 < STEPS))(lambda: phase4(s4))
 
-        for k, fn in ((5, phase5), (6, phase6), (7, phase7), (8, phase8)):
+        for k, fn in ((6, phase5), (7, phase6), (8, phase7), (9, phase8)):
             s = t - k
 
             @pl.when((s >= 0) & (s < STEPS))
@@ -605,7 +620,7 @@
 
         return carry
 
-    lax.fori_loop(1, STEPS + 8, slot, 0)
+    lax.fori_loop(1, STEPS + 9, slot, 0)
 
     offsets = (4, 3, -3, 2, -2, 1, -1, 0)
 
@@ -705,8 +720,8 @@
         dma((8, 2)),
         dma((5, 2)),
         dma((5, 2)),
-        dma((QUARTERS, 4)),
-        dma((QUARTERS, 4)),
+        dma((EARLY * QUARTERS, 4)),
+        dma((EARLY * QUARTERS, 4)),
         dma((8, 2)),
         dma((8, 2)),
         dma((STEPS, 16)),

time: 141 us -> 142 us (level)
  no operation moved by 1% of the time
where the time goes in v4:
time: 142 us; the launch traced here: 141 us
  Pallas kernels  140 us (99%)
  local copies, waits for them, and re-layouts  1.53 us (1%)
    pallas_call x1, Pallas kernels, per_device(): pl.pallas_call(block_kernel, out_shape=jax.ShapeDtypeStruct((ROWS, FEATS)...  140 us

profile of v4, /device:TPU:32, one launch (start us, length us, event | category | flops | bytes accessed | tf_op | source)
XLA Modules:
  0.0 141.5 jit_solution(4808181265986106289)
XLA Ops:
  0.0 139.9 %shard_map.100 = bf16[64,640]{1,0:T(8,128)(2,1)} custom-call(bf16[64,640]{1,0:T(8,128)(2,1)} %act.1, f32[640]{0:T(1024)} %gain.1, s32[1,1024]{1,0:T(1,128)} %bitcast.1, f32[2,1024,128]{2,1,0:T(8,128)} %constant.2.clone.table, bf16[640,768]{1,0:T(8,128)(2,1)} %w_query.1, bf16[640,512]{1,0:T(8,128)(2,1)} %w_pairs.1, bf16[640,2304]{1,0:T(8,128)(2,1)} %w_gate.1, ...), custom_call_target="tpu_custom_call" | custom-call | tf_op jit(solution)/shard_map/pallas_call | solution.py:734
  140.0 1.5 %copy.12 = bf16[64,640]{1,0:T(8,128)(2,1)} copy(bf16[64,640]{1,0:T(8,128)(2,1)} %shard_map.100) | data formatting | bytes 163840

commit v5 on v4

--- a/solution.py
+++ b/solution.py
@@ -18,7 +18,7 @@
 FEATS = D // GROUP
 WIDE = 384
 STEPS = 7
-EARLY = 2
+EARLY = 3
 UNITS = 8
 HALF = ROWS // 2
 QUARTERS = 4
@@ -53,6 +53,7 @@
     turn,
     stat,
     stat_in,
+    stat_other,
     stat_all,
     raw_all,
     rows_all,
@@ -117,12 +118,14 @@
     def dev_z(d):
         return (hid, ids_z[d])
 
-    sibling = (hid, z * 2 + 1 - core)
+    other = z * 2 + 1 - core
+    sibling = (hid, other)
     dirs = (1, -1)
     devs = ((dev_x, dev_y), (dev_y, dev_x))
 
     barrier = pltpu.get_barrier_semaphore()
     partners = [dev_x(d) for d in (1, 2, 3)] + [dev_y(d) for d in (1, 2, 3)]
+    partners += [(ids_y[d], other) for d in (1, 2, 3)]
     partners += [dev_z(1), dev_z(-1), sibling]
     for dev in partners:
         pl.semaphore_signal(barrier, inc=1, device_id=dev, device_id_type=pl.DeviceIdType.MESH)
@@ -180,6 +183,12 @@
             (dev_x, dev_y)[a](d),
         )
 
+    def other_copy(d):
+        return remote(
+            stat.at[1], stat_other.at[d], small_s.at[5 + d // 3, d % 3], small_r.at[5 + d // 3, d % 3],
+            (ids_y[d], other) if d else sibling,
+        )
+
     def pair_copy(k, d):
         if k == 0:
             src, dst, dev = pair_part.at[mod4(x + d)], pair_in.at[0, d - 1], dev_x(d)
@@ -286,47 +295,46 @@
     mean = jnp.mean(values, 1, keepdims=True)
     square = jnp.sum((values - mean) ** 2, 1, keepdims=True)
     mean, square = to_row(mean), to_row(square)
-    for a, count in ((0, FEATS), (1, FEATS * SIDE)):
-        stat[a] = jnp.where(line == 0, mean, square)
-        each(stat_copy, a, "start")
-        if a == 0:
-            kv_copy.start()
-            for s in range(EARLY):
-                for o in range(2):
-                    w_copy(s, o).start()
-            total[...] = jnp.zeros_like(total)
-        else:
-            for s in range(EARLY, STEPS):
-                for o in range(2):
-                    w_copy(s, o).start()
-            z_step(raw_all, zx, 1)
-        each(stat_copy, a, "wait")
-        means = [mean] + [stat_in[a, d, 0:1] for d in range(3)]
-        squares = [square] + [stat_in[a, d, 1:2] for d in range(3)]
+    def merge(count, tiles):
+        means = [tile[0:1] for tile in tiles]
+        squares = [tile[1:2] for tile in tiles]
         mean = (means[0] + means[1] + means[2] + means[3]) * 0.25
         square = squares[0] + squares[1] + squares[2] + squares[3]
         for one in means:
             square += count * (one - mean) ** 2
-    scale = lax.rsqrt(square * (1.0 / D) + EPSILON)
-    stat_all[z, core] = jnp.where(line == 0, mean, scale)
-    stat_sib = remote(
-        stat_all.at[z, core], stat_all.at[z, core], zt_s.at[0, 0], zt_r.at[0, 0], sibling
-    )
-    stat_sib.start()
-    normed = norm(act[...], stat_all[z, core])
-    stat_sib.wait()
+        return mean, square
+
+    def finish(tiles):
+        mean, square = merge(FEATS * SIDE, tiles)
+        return jnp.where(line == 0, mean, lax.rsqrt(square * (1.0 / D) + EPSILON))
+
+    stat[0] = jnp.where(line == 0, mean, square)
+    each(stat_copy, 0, "start")
+    kv_copy.start()
+    for s in range(EARLY):
+        for o in range(2):
+            w_copy(s, o).start()
+    total[...] = jnp.zeros_like(total)
+    each(stat_copy, 0, "wait")
+    mean, square = merge(FEATS, [stat[0]] + [stat_in[0, d] for d in range(3)])
+    stat[1] = jnp.where(line == 0, mean, square)
+    each(stat_copy, 1, "start")
+    for d in range(SIDE):
+        other_copy(d).start()
+    z_step(raw_all, zx, 1)
+    each(stat_copy, 1, "wait")
+    for d in range(SIDE):
+        other_copy(d).wait()
+    stat_all[z, core] = finish([stat[1]] + [stat_in[1, d] for d in range(3)])
+    stat_all[z, 1 - core] = finish([stat_other[d] for d in range(SIDE)])
     for i in range(2):
         stat_z(1, i).start()
+    normed = norm(act[...], stat_all[z, core])
     kv_copy.wait()
     pairs = jnp.dot(normed, w_kv[...], preferred_element_type=F32).astype(BF16)
     for q in range(4):
         pair_part[q] = pairs[:, q * 128 : (q + 1) * 128]
     each(pair_copy, 0, "start")
-    for i in range(2):
-        for copy in turn_copies(i):
-            copy.start()
-    for u in range(UNITS):
-        wb_copy(u).start()
     for s in range(EARLY):
         for o in range(2):
             w_copy(s, o).wait()
@@ -335,7 +343,7 @@
     turned = 1 - 2 * (z % 2)
     order = (pair, mod4(pair - turned), mod4(pair + turned), mod4(pair + 2))
 
-    def first_products(j):
+    def first_rows(j):
         g = order[j]
 
         def one(k, carry):
@@ -343,15 +351,23 @@
             return carry
 
         lax.fori_loop(0, QUARTERS, one, 0)
-        for s in range(EARLY):
+
+    def first_products(j, steps):
+        g = order[j]
+        for s in steps:
             products(s, g)
             for o, i in both:
                 quarter_copy(s, j, g, o, i).start()
 
-    z_step(raw_all, zx, 2)
     stat_step(1)
     sib_wait(raw_all, zx, 0, 1, -1)
-    first_products(0)
+    first_rows(0)
+    first_products(0, (0,))
+    z_step(raw_all, zx, 2)
+    first_products(0, range(1, EARLY))
+    for s in range(EARLY, STEPS):
+        for o in range(2):
+            w_copy(s, o).start()
     each(pair_copy, 0, "wait")
     pair_sum[...] = (
         pair_part[x].astype(F32)
@@ -363,7 +379,13 @@
     z_step(raw_all, zx, 3)
     stat_step(2)
     sib_wait(raw_all, zx, 2, -2)
-    first_products(1)
+    first_rows(1)
+    first_products(1, range(EARLY))
+    for i in range(2):
+        for copy in turn_copies(i):
+            copy.start()
+    for u in range(UNITS):
+        wb_copy(u).start()
     each(pair_copy, 1, "wait")
     pair_all[x] = (
         pair_sum[...].astype(F32)
@@ -375,10 +397,12 @@
     z_step(raw_all, zx, 4)
     stat_step(3)
     sib_wait(raw_all, zx, 3, -3)
-    first_products(2)
+    first_rows(2)
+    first_products(2, range(EARLY))
     stat_step(4)
     sib_wait(raw_all, zx, 4)
-    first_products(3)
+    first_rows(3)
+    first_products(3, range(EARLY))
     each(pair_copy, 2, "wait")
     for i in range(2):
         for copy in turn_copies(i):
@@ -639,11 +663,14 @@
         at = mod8(z + offsets[k])
         return remote(sib_out.at[at], sib_in.at[at], zr_s.at[k], zr_r.at[k], sibling)
 
-    for k in range(RING):
-        at = mod8(z + offsets[k])
-        for h in range(2):
-            sib_out[at, h * HALF : (h + 1) * HALF] = half_rows(at * 2 + 1 - core, h).astype(BF16)
-        sib_sum(k).start()
+    def sib_send(*which):
+        for k in which:
+            at = mod8(z + offsets[k])
+            for h in range(2):
+                sib_out[at, h * HALF : (h + 1) * HALF] = half_rows(at * 2 + 1 - core, h).astype(BF16)
+            sib_sum(k).start()
+
+    sib_send(0, 1, 2)
 
     def chip_sum(k, h):
         at = mod8(z + offsets[k])
@@ -659,6 +686,7 @@
     for i in range(2):
         ring_out[0, i, i] = chip_sum(0, i).astype(BF16)
         ring_copy(0, i, i).start()
+    sib_send(3, 4)
     for j in (1, 2, 3):
         for i in range(2):
             sib_sum(2 * j - 1 + i).wait()
@@ -671,6 +699,8 @@
                     here += ring_in[j - 1, i, h].astype(F32)
                 ring_out[j, i, h] = here.astype(BF16)
                 ring_copy(j, i, h).start()
+        if j < 3:
+            sib_send(*((5, 6), (7,))[j - 1])
     sib_sum(7).wait()
     for h in range(2):
         here = chip_sum(7, h) + act[h * HALF : (h + 1) * HALF].astype(F32)
@@ -691,6 +721,7 @@
         pltpu.VMEM((2, 2, ROWS, 128), F32),
         pltpu.VMEM((2, 8, 128), F32),
         pltpu.VMEM((2, 3, 8, 128), F32),
+        pltpu.VMEM((4, 8, 128), F32),
         pltpu.VMEM((RING, 2, 8, 128), F32),
         pltpu.VMEM((GROUP, ROWS, FEATS), BF16),
         pltpu.VMEM((GROUP, ROWS, FEATS), BF16),
@@ -714,8 +745,8 @@
         dma((STEPS, 2)),
         dma((UNITS,)),
         dma((11,)),
-        dma((5, 3)),
-        dma((5, 3)),
+        dma((7, 3)),
+        dma((7, 3)),
         dma((8, 2)),
         dma((8, 2)),
         dma((5, 2)),

time: 142 us -> 141 us (level)
  no operation moved by 1% of the time
where the time goes in v5:
time: 141 us
  Pallas kernels  139 us (99%)
  local copies, waits for them, and re-layouts  1.53 us (1%)
    pallas_call x1, Pallas kernels, per_device(): pl.pallas_call(block_kernel, out_shape=jax.ShapeDtypeStruct((ROWS, FEATS)...  139 us

profile of v5, /device:TPU:32, one launch (start us, length us, event | category | flops | bytes accessed | tf_op | source)
XLA Modules:
  0.0 140.7 jit_solution(17933597785207532066)
XLA Ops:
  0.0 139.2 %shard_map.100 = bf16[64,640]{1,0:T(8,128)(2,1)} custom-call(bf16[64,640]{1,0:T(8,128)(2,1)} %act.1, f32[640]{0:T(1024)} %gain.1, s32[1,1024]{1,0:T(1,128)} %bitcast.1, f32[2,1024,128]{2,1,0:T(8,128)} %constant.2.clone.table, bf16[640,768]{1,0:T(8,128)(2,1)} %w_query.1, bf16[640,512]{1,0:T(8,128)(2,1)} %w_pairs.1, bf16[640,2304]{1,0:T(8,128)(2,1)} %w_gate.1, ...), custom_call_target="tpu_custom_call" | custom-call | tf_op jit(solution)/shard_map/pallas_call | solution.py:765
  139.2 1.5 %copy.12 = bf16[64,640]{1,0:T(8,128)(2,1)} copy(bf16[64,640]{1,0:T(8,128)(2,1)} %shard_map.100) | data formatting | bytes 163840

commit v6 on v5

--- a/solution.py
+++ b/solution.py
@@ -469,9 +469,7 @@
 
         for o, i in both:
             first, size = near1[i]
-            part[s, o, :, first : first + size] = added(
-                part[s, o, :, first : first + size], land1[s, o, i, :, 2 - 2 * i : 4 - 2 * i]
-            ).astype(BF16)
+            part[s, o, :, first : first + size] += land1[s, o, i, :, 2 - 2 * i : 4 - 2 * i]
             rs_copy(s, o, 1, i).start()
 
     def phase2(s):
@@ -497,7 +495,7 @@
         for o, i in both:
             rs_copy(s, o, 2, i).wait()
             first = near2[i][0]
-            half_sum[s, o, first] = added(half_sum[s, o, first], land2[s, o, i, 1 - i]).astype(BF16)
+            half_sum[s, o, first] += land2[s, o, i, 1 - i]
             rs_copy(s, o, 3, i).start()
 
     def attend(left, right):
@@ -604,34 +602,42 @@
             gather_copy(u, o, 2, i).wait()
             gather_copy(u, o, 3, i).start()
 
+    def accumulate(u, count):
+        weights = w_back[pl.ds(u, count)].reshape(count * WIDE, FEATS)
+        for o in range(2):
+            for p in range(2):
+                rows = [
+                    mixed[u + k, o, 2 * p : 2 * p + 2].reshape(2 * SIDE * HALF, WIDE)
+                    for k in range(count)
+                ]
+                total[o, p * 256 : (p + 1) * 256] += jnp.dot(
+                    jnp.concatenate(rows, 1), weights, preferred_element_type=F32
+                )
+
     def phase8(u):
-        for o in range(2):
-            for i in range(2):
-                gather_copy(u, o, 3, i).wait()
-            for p in range(2):
-                rows = mixed[u, o, 2 * p : 2 * p + 2].reshape(2 * SIDE * HALF, WIDE)
-                total[o, p * 256 : (p + 1) * 256] += jnp.dot(
-                    rows, w_back[u], preferred_element_type=F32
-                )
+        for o, i in both:
+            gather_copy(u, o, 3, i).wait()
+        pl.when((u % 2 == 1) & (u < 6))(lambda: accumulate(u - 1, 2))
+        pl.when(u >= 6)(lambda: accumulate(u, 1))
 
     def slot(t, carry):
         pl.when((t >= EARLY) & (t < STEPS))(lambda: phase0(t))
-        for k, fn in ((1, phase1), (3, phase2), (4, phase3)):
+        for k, fn in ((2, phase1), (4, phase2), (5, phase3)):
             s = t - k
             pl.when((s >= 0) & (s < STEPS))(lambda fn=fn, s=s: fn(s))
 
         for j in range(1, 5):
 
-            @pl.when(t == j)
+            @pl.when(t == j + 1)
             def _(j=j):
                 z_step(kv_all, zk, j)
                 if j == 4:
                     sib_wait(kv_all, zk, 0, 1, -1, 2, -2, 3, -3, 4)
 
-        s4 = t - 5
+        s4 = t - 6
         pl.when((s4 >= 0) & (s4 < STEPS))(lambda: phase4(s4))
 
-        for k, fn in ((6, phase5), (7, phase6), (8, phase7), (9, phase8)):
+        for k, fn in ((7, phase5), (8, phase6), (9, phase7), (10, phase8)):
             s = t - k
 
             @pl.when((s >= 0) & (s < STEPS))
@@ -644,7 +650,7 @@
 
         return carry
 
-    lax.fori_loop(1, STEPS + 9, slot, 0)
+    lax.fori_loop(2, STEPS + 10, slot, 0)
 
     offsets = (4, 3, -3, 2, -2, 1, -1, 0)
 

time: 141 us -> 140 us (level)
  no operation moved by 1% of the time
where the time goes in v6:
time: 140 us
  Pallas kernels  138 us (99%)
  local copies, waits for them, and re-layouts  1.53 us (1%)
    pallas_call x1, Pallas kernels, per_device(): pl.pallas_call(block_kernel, out_shape=jax.ShapeDtypeStruct((ROWS, FEATS)...  138 us

profile of v6, /device:TPU:32, one launch (start us, length us, event | category | flops | bytes accessed | tf_op | source)
XLA Modules:
  0.0 139.9 jit_solution(1687289213434443439)
XLA Ops:
  0.0 138.4 %shard_map.100 = bf16[64,640]{1,0:T(8,128)(2,1)} custom-call(bf16[64,640]{1,0:T(8,128)(2,1)} %act.1, f32[640]{0:T(1024)} %gain.1, s32[1,1024]{1,0:T(1,128)} %bitcast.1, f32[2,1024,128]{2,1,0:T(8,128)} %constant.2.clone.table, bf16[640,768]{1,0:T(8,128)(2,1)} %w_query.1, bf16[640,512]{1,0:T(8,128)(2,1)} %w_pairs.1, bf16[640,2304]{1,0:T(8,128)(2,1)} %w_gate.1, ...), custom_call_target="tpu_custom_call" | custom-call | tf_op jit(solution)/shard_map/pallas_call | solution.py:771
  138.4 1.5 %copy.12 = bf16[64,640]{1,0:T(8,128)(2,1)} copy(bf16[64,640]{1,0:T(8,128)(2,1)} %shard_map.100) | data formatting | bytes 163840

commit v7 on v6

--- a/solution.py
+++ b/solution.py
@@ -19,6 +19,7 @@
 WIDE = 384
 STEPS = 7
 EARLY = 3
+PAIRED = 6
 UNITS = 8
 HALF = ROWS // 2
 QUARTERS = 4
@@ -65,7 +66,7 @@
     part,
     land1,
     last1,
-    half_sum,
+    near_sum,
     land2,
     last2,
     mixed,
@@ -249,8 +250,8 @@
     def quarter_copy(s, j, g, o, i):
         at = o * 2 + i
         return remote(
-            part.at[s, o, g, pl.ds((6, 10)[i], 4)],
-            land1.at[s, o, i, g],
+            part.at[s, o, pl.ds((6, 10)[i], 4), g],
+            land1.at[s, o, i, :, g],
             rq_s.at[s * QUARTERS + j, at],
             rq_r.at[s * QUARTERS + j, at],
             devs[o][0](dirs[i]),
@@ -270,7 +271,7 @@
         for h in range(GROUP):
             block = res[h * QUARTER : (h + 1) * QUARTER]
             for o in range(2):
-                part[s, o, g, places[o][h]] = block[:, o * WIDE : (o + 1) * WIDE]
+                part[s, o, places[o][h], g] = block[:, o * WIDE : (o + 1) * WIDE]
 
     eye = lax.broadcasted_iota(jnp.int32, (ROWS, 128), 0) == lax.broadcasted_iota(
         jnp.int32, (ROWS, 128), 1
@@ -422,16 +423,16 @@
 
     far1 = ((6, 4), (10, 4))
     near1 = ((4, 2), (14, 2))
-    far2 = ((3, 2), (5, 2))
-    near2 = ((2, 1), (7, 1))
 
     def rs_copy(s, o, k, i):
-        first, size = (far1, near1, far2, near2)[k][i]
         at = o * 8 + k * 2 + i
         if k < 2:
-            src = part.at[s, o, :, pl.ds(first, size)]
+            first, size = (far1, near1)[k][i]
+            src = part.at[s, o, pl.ds(first, size)]
+        elif k == 2:
+            src = near_sum.at[s, o, pl.ds((6, 10)[i], 4)]
         else:
-            src = half_sum.at[s, o, pl.ds(first, size)]
+            src = near_sum.at[s, o, pl.ds((4, 14)[i], 2)]
         return remote(
             src,
             (land1, last1, land2, last2)[k].at[s, o, i],
@@ -469,7 +470,7 @@
 
         for o, i in both:
             first, size = near1[i]
-            part[s, o, :, first : first + size] += land1[s, o, i, :, 2 - 2 * i : 4 - 2 * i]
+            part[s, o, first : first + size] += land1[s, o, i, 2 - 2 * i : 4 - 2 * i]
             rs_copy(s, o, 1, i).start()
 
     def phase2(s):
@@ -477,25 +478,20 @@
             for i in range(2):
                 rs_copy(s, o, 1, i).wait()
             for i in range(2):
-                cut = slice(2 - 2 * i, 4 - 2 * i)
                 res = added(
-                    part[s, o, :, 2 * i : 2 * i + 2],
+                    part[s, o, 2 * i : 2 * i + 2],
                     last1[s, o, i],
-                    land1[s, o, 1 - i, :, cut],
+                    land1[s, o, 1 - i, 2 - 2 * i : 4 - 2 * i],
                 ).astype(BF16)
-                for b in range(2):
-                    for r in range(2):
-                        half_sum[s, o, (2 * i + b) * 2 + r] = res[2 * r : 2 * r + 2, b].reshape(
-                            HALF, WIDE
-                        )
+                near_sum[s, o, 8 * i : 8 * i + 8] = res.reshape(2 * QUARTERS, QUARTER, WIDE)
             for i in range(2):
                 rs_copy(s, o, 2, i).start()
 
     def phase3(s):
         for o, i in both:
             rs_copy(s, o, 2, i).wait()
-            first = near2[i][0]
-            half_sum[s, o, first] += land2[s, o, i, 1 - i]
+            first = (4, 14)[i]
+            near_sum[s, o, first : first + 2] += land2[s, o, i, 2 - 2 * i : 4 - 2 * i]
             rs_copy(s, o, 3, i).start()
 
     def attend(left, right):
@@ -532,25 +528,35 @@
         return jnp.concatenate(pieces[:3], 1), jnp.concatenate(pieces[3:], 1)
 
     def put(u, block):
-        mixed[u, 0, 0, 0] = block[0:HALF]
-        mixed[u, 1, 0, 0] = block[HALF:ROWS]
-
-    def gather_copy(u, o, k, i):
+        for o in range(2):
+            mixed[u // 2, o, 0, 0, u % 2] = block[o * HALF : (o + 1) * HALF]
+
+    def gather_copy(u, n, o, k, i):
         d = dirs[i]
         away, near = (3, 1)[i], (3, 1)[i]
         dev = devs[o][k // 2](d)
+        pair = mixed.at[u // 2, o]
+        which = pl.ds(u % 2, 1) if n == 1 else pl.ds(0, 2)
         if k == 0:
-            src, dst = mixed.at[u, o, 0, 0], mixed.at[u, o, 0, away]
+            src, dst = pair.at[0, 0, which], pair.at[0, away, which]
         elif k == 1:
             rows = pl.ds(i * QUARTER, QUARTER)
-            src, dst = mixed.at[u, o, 0, near, rows], mixed.at[u, o, 0, 2, rows]
+            src, dst = pair.at[0, near, which, rows], pair.at[0, 2, which, rows]
         elif k == 2:
-            src, dst = mixed.at[u, o, 0], mixed.at[u, o, away]
+            src, dst = pair.at[0, :, which], pair.at[away, :, which]
         else:
             cut = pl.ds(2 * i, 2)
-            src, dst = mixed.at[u, o, near, cut], mixed.at[u, o, 2, cut]
+            src, dst = pair.at[near, cut, which], pair.at[2, cut, which]
         at = o * 8 + k * 2 + i
         return remote(src, dst, ag_s.at[u, at], ag_r.at[u, at], dev)
+
+    def by_units(u, fn):
+        pl.when((u % 2 == 1) & (u < PAIRED))(lambda: fn(u - 1, 2))
+        pl.when(u >= PAIRED)(lambda: fn(u, 1))
+
+    def gather_first(u, n):
+        for o, i in both:
+            gather_copy(u, n, o, 0, i).start()
 
     def phase4(s):
         sums = []
@@ -560,9 +566,11 @@
             sums.append(
                 jnp.concatenate(
                     [
-                        half_sum[s, o, i].astype(F32)
-                        + last2[s, o, i, 0].astype(F32)
-                        + land2[s, o, 1 - i, 1 - i].astype(F32)
+                        added(
+                            near_sum[s, o, 2 * i : 2 * i + 2],
+                            last2[s, o, i],
+                            land2[s, o, 1 - i, 2 - 2 * i : 4 - 2 * i],
+                        ).reshape(HALF, WIDE)
                         for i in range(2)
                     ],
                     0,
@@ -574,51 +582,47 @@
             left, right = attend(*sums)
             put(0, left)
             put(1, right)
-            for u in range(2):
-                for o, i in both:
-                    gather_copy(u, o, 0, i).start()
+            gather_first(0, 2)
 
         @pl.when(s > 0)
         def _():
             gate, up = sums
             put(s + 1, (gate / (1.0 + jnp.exp(-gate)) * up).astype(BF16))
-            for o, i in both:
-                gather_copy(s + 1, o, 0, i).start()
-
-    def phase5(u):
+            by_units(s + 1, gather_first)
+
+    def phase5(u, n):
         for o, i in both:
-            gather_copy(u, o, 0, i).wait()
-            gather_copy(u, o, 1, i).start()
-
-    def phase6(u):
+            gather_copy(u, n, o, 0, i).wait()
+            gather_copy(u, n, o, 1, i).start()
+
+    def phase6(u, n):
         for o in range(2):
             for i in range(2):
-                gather_copy(u, o, 1, i).wait()
+                gather_copy(u, n, o, 1, i).wait()
             for i in range(2):
-                gather_copy(u, o, 2, i).start()
-
-    def phase7(u):
+                gather_copy(u, n, o, 2, i).start()
+
+    def phase7(u, n):
         for o, i in both:
-            gather_copy(u, o, 2, i).wait()
-            gather_copy(u, o, 3, i).start()
+            gather_copy(u, n, o, 2, i).wait()
+            gather_copy(u, n, o, 3, i).start()
 
     def accumulate(u, count):
         weights = w_back[pl.ds(u, count)].reshape(count * WIDE, FEATS)
         for o in range(2):
             for p in range(2):
                 rows = [
-                    mixed[u + k, o, 2 * p : 2 * p + 2].reshape(2 * SIDE * HALF, WIDE)
-                    for k in range(count)
+                    mixed[u // 2, o, 2 * p : 2 * p + 2, :, one].reshape(2 * SIDE * HALF, WIDE)
+                    for one in (range(2) if count == 2 else (u % 2,))
                 ]
                 total[o, p * 256 : (p + 1) * 256] += jnp.dot(
                     jnp.concatenate(rows, 1), weights, preferred_element_type=F32
                 )
 
-    def phase8(u):
+    def phase8(u, n):
         for o, i in both:
-            gather_copy(u, o, 3, i).wait()
-        pl.when((u % 2 == 1) & (u < 6))(lambda: accumulate(u - 1, 2))
-        pl.when(u >= 6)(lambda: accumulate(u, 1))
+            gather_copy(u, n, o, 3, i).wait()
+        accumulate(u, n)
 
     def slot(t, carry):
         pl.when((t >= EARLY) & (t < STEPS))(lambda: phase0(t))
@@ -642,11 +646,7 @@
 
             @pl.when((s >= 0) & (s < STEPS))
             def _(fn=fn, s=s):
-                def unit(u, c):
-                    fn(u)
-                    return c
-
-                lax.fori_loop(jnp.where(s == 0, 0, s + 1), s + 2, unit, 0)
+                by_units(s + 1, fn)
 
         return carry
 
@@ -736,13 +736,13 @@
         pltpu.VMEM((ROWS, 128), BF16),
         pltpu.VMEM((4, ROWS, 128), BF16),
         pltpu.VMEM((GROUP, ROWS, 512), BF16),
-        pltpu.VMEM((STEPS, 2, QUARTERS, GROUP, QUARTER, WIDE), BF16),
-        pltpu.VMEM((STEPS, 2, 2, QUARTERS, 4, QUARTER, WIDE), BF16),
-        pltpu.VMEM((STEPS, 2, 2, QUARTERS, 2, QUARTER, WIDE), BF16),
-        pltpu.VMEM((STEPS, 2, 2 * SIDE, HALF, WIDE), BF16),
-        pltpu.VMEM((STEPS, 2, 2, 2, HALF, WIDE), BF16),
-        pltpu.VMEM((STEPS, 2, 2, 1, HALF, WIDE), BF16),
-        pltpu.VMEM((UNITS, 2, SIDE, SIDE, HALF, WIDE), BF16),
+        pltpu.VMEM((STEPS, 2, GROUP, QUARTERS, QUARTER, WIDE), BF16),
+        pltpu.VMEM((STEPS, 2, 2, 4, QUARTERS, QUARTER, WIDE), BF16),
+        pltpu.VMEM((STEPS, 2, 2, 2, QUARTERS, QUARTER, WIDE), BF16),
+        pltpu.VMEM((STEPS, 2, SIDE * QUARTERS, QUARTER, WIDE), BF16),
+        pltpu.VMEM((STEPS, 2, 2, QUARTERS, QUARTER, WIDE), BF16),
+        pltpu.VMEM((STEPS, 2, 2, 2, QUARTER, WIDE), BF16),
+        pltpu.VMEM((UNITS // 2, 2, SIDE, SIDE, 2, HALF, WIDE), BF16),
         pltpu.VMEM((2, GROUP * HALF, FEATS), F32),
         pltpu.VMEM((RING, ROWS, FEATS), BF16),
         pltpu.VMEM((RING, ROWS, FEATS), BF16),

time: 140 us -> 141 us (level)
  no operation moved by 1% of the time
where the time goes in v7:
time: 141 us
  Pallas kernels  139 us (99%)
  local copies, waits for them, and re-layouts  1.53 us (1%)
    pallas_call x1, Pallas kernels, per_device(): pl.pallas_call(block_kernel, out_shape=jax.ShapeDtypeStruct((ROWS, FEATS)...  139 us

profile of v7, /device:TPU:32, one launch (start us, length us, event | category | flops | bytes accessed | tf_op | source)
XLA Modules:
  0.0 140.7 jit_solution(13389565642357207264)
XLA Ops:
  0.0 139.2 %shard_map.100 = bf16[64,640]{1,0:T(8,128)(2,1)} custom-call(bf16[64,640]{1,0:T(8,128)(2,1)} %act.1, f32[640]{0:T(1024)} %gain.1, s32[1,1024]{1,0:T(1,128)} %bitcast.1, f32[2,1024,128]{2,1,0:T(8,128)} %constant.2.clone.table, bf16[640,768]{1,0:T(8,128)(2,1)} %w_query.1, bf16[640,512]{1,0:T(8,128)(2,1)} %w_pairs.1, bf16[640,2304]{1,0:T(8,128)(2,1)} %w_gate.1, ...), custom_call_target="tpu_custom_call" | custom-call | tf_op jit(solution)/shard_map/pallas_call | solution.py:771
  139.2 1.5 %copy.12 = bf16[64,640]{1,0:T(8,128)(2,1)} copy(bf16[64,640]{1,0:T(8,128)(2,1)} %shard_map.100) | data formatting | bytes 163840

commit v8 on v7

--- a/solution.py
+++ b/solution.py
@@ -19,7 +19,7 @@
 WIDE = 384
 STEPS = 7
 EARLY = 3
-PAIRED = 6
+PAIRED = 2
 UNITS = 8
 HALF = ROWS // 2
 QUARTERS = 4
@@ -176,6 +176,10 @@
 
     kv_copy = pltpu.make_async_copy(w_pairs, w_kv, m_sem.at[0])
 
+    kv_copy.start(priority=1)
+    for s in range(EARLY):
+        for o in range(2):
+            w_copy(s, o).start(priority=1)
     pl.semaphore_wait(barrier, len(partners))
 
     def stat_copy(a, d):
@@ -311,10 +315,6 @@
 
     stat[0] = jnp.where(line == 0, mean, square)
     each(stat_copy, 0, "start")
-    kv_copy.start()
-    for s in range(EARLY):
-        for o in range(2):
-            w_copy(s, o).start()
     total[...] = jnp.zeros_like(total)
     each(stat_copy, 0, "wait")
     mean, square = merge(FEATS, [stat[0]] + [stat_in[0, d] for d in range(3)])
@@ -368,7 +368,7 @@
     first_products(0, range(1, EARLY))
     for s in range(EARLY, STEPS):
         for o in range(2):
-            w_copy(s, o).start()
+            w_copy(s, o).start(priority=1)
     each(pair_copy, 0, "wait")
     pair_sum[...] = (
         pair_part[x].astype(F32)
@@ -384,9 +384,9 @@
     first_products(1, range(EARLY))
     for i in range(2):
         for copy in turn_copies(i):
-            copy.start()
+            copy.start(priority=1)
     for u in range(UNITS):
-        wb_copy(u).start()
+        wb_copy(u).start(priority=1)
     each(pair_copy, 1, "wait")
     pair_all[x] = (
         pair_sum[...].astype(F32)
@@ -654,16 +654,16 @@
 
     offsets = (4, 3, -3, 2, -2, 1, -1, 0)
 
-    def half_rows(block, h):
+    def some_rows(block, k):
         g = block // SIDE
         o = g // 2
         px = mod4(block % SIDE - x)
-        pieces = []
-        for k in (2 * h, 2 * h + 1):
-            place = jnp.where(o == 0, rel_y[k] * SIDE + px, px * SIDE + rel_y[k])
-            first = pl.multiple_of(place * HALF + (g % 2) * QUARTER, QUARTER)
-            pieces.append(total[o, pl.ds(first, QUARTER)])
-        return jnp.concatenate(pieces, 0)
+        place = jnp.where(o == 0, rel_y[k] * SIDE + px, px * SIDE + rel_y[k])
+        first = pl.multiple_of(place * HALF + (g % 2) * QUARTER, QUARTER)
+        return total[o, pl.ds(first, QUARTER)]
+
+    def span(k):
+        return slice(k * QUARTER, (k + 1) * QUARTER)
 
     def sib_sum(k):
         at = mod8(z + offsets[k])
@@ -672,48 +672,49 @@
     def sib_send(*which):
         for k in which:
             at = mod8(z + offsets[k])
-            for h in range(2):
-                sib_out[at, h * HALF : (h + 1) * HALF] = half_rows(at * 2 + 1 - core, h).astype(BF16)
+            for q in range(4):
+                sib_out[at, span(q)] = some_rows(at * 2 + 1 - core, q).astype(BF16)
             sib_sum(k).start()
 
     sib_send(0, 1, 2)
 
-    def chip_sum(k, h):
+    def chip_sum(k, q):
         at = mod8(z + offsets[k])
-        return half_rows(at * 2 + core, h) + sib_in[at, h * HALF : (h + 1) * HALF].astype(F32)
-
-    def ring_copy(j, i, h):
-        at = 8 + j * 4 + i * 2 + h
+        return some_rows(at * 2 + core, q) + sib_in[at, span(q)].astype(F32)
+
+    def ring_copy(j, i, q):
+        at = 8 + (j * 2 + i) * 4 + q
         return remote(
-            ring_out.at[j, i, h], ring_in.at[j, i, h], zr_s.at[at], zr_r.at[at], dev_z(dirs[i])
+            ring_out.at[j, i, q], ring_in.at[j, i, q], zr_s.at[at], zr_r.at[at], dev_z(dirs[i])
         )
 
     sib_sum(0).wait()
-    for i in range(2):
-        ring_out[0, i, i] = chip_sum(0, i).astype(BF16)
-        ring_copy(0, i, i).start()
+    for q in range(2):
+        for i in range(2):
+            ring_out[0, i, 2 * i + q] = chip_sum(0, 2 * i + q).astype(BF16)
+            ring_copy(0, i, 2 * i + q).start()
     sib_send(3, 4)
     for j in (1, 2, 3):
         for i in range(2):
             sib_sum(2 * j - 1 + i).wait()
-        for turn_of in range(2):
+        for turn_of in range(4):
             for i in range(2):
-                h = (1 - i, i)[turn_of]
-                here = chip_sum(2 * j - 1 + i, h)
-                if j > 1 or h == i:
-                    ring_copy(j - 1, i, h).wait()
-                    here += ring_in[j - 1, i, h].astype(F32)
-                ring_out[j, i, h] = here.astype(BF16)
-                ring_copy(j, i, h).start()
+                q = (2 * (1 - i) + turn_of) % 4
+                here = chip_sum(2 * j - 1 + i, q)
+                if j > 1 or q // 2 == i:
+                    ring_copy(j - 1, i, q).wait()
+                    here += ring_in[j - 1, i, q].astype(F32)
+                ring_out[j, i, q] = here.astype(BF16)
+                ring_copy(j, i, q).start()
         if j < 3:
             sib_send(*((5, 6), (7,))[j - 1])
     sib_sum(7).wait()
-    for h in range(2):
-        here = chip_sum(7, h) + act[h * HALF : (h + 1) * HALF].astype(F32)
+    for q in (2, 0, 3, 1):
+        here = chip_sum(7, q) + act[span(q)].astype(F32)
         for i in range(2):
-            ring_copy(3, i, h).wait()
-            here += ring_in[3, i, h].astype(F32)
-        out[h * HALF : (h + 1) * HALF] = here.astype(BF16)
+            ring_copy(3, i, q).wait()
+            here += ring_in[3, i, q].astype(F32)
+        out[span(q)] = here.astype(BF16)
 
 
 def per_device(activations, ln_gain, segments, w_query, w_key_value, w_gate, w_up, w_out, w_down):
@@ -746,8 +747,8 @@
         pltpu.VMEM((2, GROUP * HALF, FEATS), F32),
         pltpu.VMEM((RING, ROWS, FEATS), BF16),
         pltpu.VMEM((RING, ROWS, FEATS), BF16),
-        pltpu.VMEM((4, 2, 2, HALF, FEATS), BF16),
-        pltpu.VMEM((4, 2, 2, HALF, FEATS), BF16),
+        pltpu.VMEM((4, 2, 4, QUARTER, FEATS), BF16),
+        pltpu.VMEM((4, 2, 4, QUARTER, FEATS), BF16),
         dma((STEPS, 2)),
         dma((UNITS,)),
         dma((11,)),
@@ -765,8 +766,8 @@
         dma((STEPS, 16)),
         dma((UNITS, 16)),
         dma((UNITS, 16)),
-        dma((24,)),
-        dma((24,)),
+        dma((40,)),
+        dma((40,)),
     ]
     return pl.pallas_call(
         block_kernel,

time: 141 us -> 140 us (level)
  no operation moved by 1% of the time
where the time goes in v8:
time: 140 us; the launch traced here: 139 us
  Pallas kernels  138 us (99%)
  local copies, waits for them, and re-layouts  1.53 us (1%)
    pallas_call x1, Pallas kernels, per_device(): pl.pallas_call(block_kernel, out_shape=jax.ShapeDtypeStruct((ROWS, FEATS)...  138 us

profile of v8, /device:TPU:32, one launch (start us, length us, event | category | flops | bytes accessed | tf_op | source)
XLA Modules:
  0.0 139.4 jit_solution(15975475695370113175)
XLA Ops:
  0.0 137.9 %shard_map.100 = bf16[64,640]{1,0:T(8,128)(2,1)} custom-call(bf16[64,640]{1,0:T(8,128)(2,1)} %act.1, f32[640]{0:T(1024)} %gain.1, s32[1,1024]{1,0:T(1,128)} %bitcast.1, f32[2,1024,128]{2,1,0:T(8,128)} %constant.2.clone.table, bf16[640,768]{1,0:T(8,128)(2,1)} %w_query.1, bf16[640,512]{1,0:T(8,128)(2,1)} %w_pairs.1, bf16[640,2304]{1,0:T(8,128)(2,1)} %w_gate.1, ...), custom_call_target="tpu_custom_call" | custom-call | tf_op jit(solution)/shard_map/pallas_call | solution.py:772
  137.9 1.5 %copy.12 = bf16[64,640]{1,0:T(8,128)(2,1)} copy(bf16[64,640]{1,0:T(8,128)(2,1)} %shard_map.100) | data formatting | bytes 163840

commit v9 on v8

--- a/solution.py
+++ b/solution.py
@@ -19,7 +19,6 @@
 WIDE = 384
 STEPS = 7
 EARLY = 3
-PAIRED = 2
 UNITS = 8
 HALF = ROWS // 2
 QUARTERS = 4
@@ -62,6 +61,7 @@
     pair_in,
     pair_sum,
     pair_all,
+    heads,
     kv_all,
     part,
     land1,
@@ -251,6 +251,12 @@
             if j < 3 + (i == 0):
                 stat_z(j + 1, i).start()
 
+    def added(first, *rest):
+        res = first.astype(F32)
+        for one in rest:
+            res += one.astype(F32)
+        return res
+
     def quarter_copy(s, j, g, o, i):
         at = o * 2 + i
         return remote(
@@ -342,68 +348,69 @@
 
     pair = z // 2
     turned = 1 - 2 * (z % 2)
-    order = (pair, mod4(pair - turned), mod4(pair + turned), mod4(pair + 2))
-
-    def first_rows(j):
-        g = order[j]
-
-        def one(k, carry):
+    def order(j):
+        step = jnp.where(j == 3, 2, jnp.where(j == 0, 0, jnp.where(j == 1, -turned, turned)))
+        return mod4(pair + step)
+
+    def pair_add(own, a):
+        return added(own, pair_in[a, 0], pair_in[a, 1], pair_in[a, 2]).astype(BF16)
+
+    def early(j, carry):
+        @pl.when(j == 0)
+        def _():
+            stat_step(1)
+            sib_wait(raw_all, zx, 0, 1, -1)
+
+        @pl.when(j == 1)
+        def _():
+            for s in range(EARLY, STEPS):
+                for o in range(2):
+                    w_copy(s, o).start(priority=1)
+            each(pair_copy, 0, "wait")
+            pair_sum[...] = pair_add(pair_part[x], 0)
+            each(pair_copy, 1, "start")
+            z_step(raw_all, zx, 3)
+            stat_step(2)
+            sib_wait(raw_all, zx, 2, -2)
+
+        @pl.when(j == 2)
+        def _():
+            for i in range(2):
+                for copy in turn_copies(i):
+                    copy.start(priority=1)
+            for u in range(UNITS):
+                wb_copy(u).start(priority=1)
+            each(pair_copy, 1, "wait")
+            pair_all[x] = pair_add(pair_sum[...], 1)
+            each(pair_copy, 2, "start")
+            z_step(raw_all, zx, 4)
+            stat_step(3)
+            sib_wait(raw_all, zx, 3, -3)
+
+        @pl.when(j == 3)
+        def _():
+            stat_step(4)
+            sib_wait(raw_all, zx, 4)
+
+        g = order(j)
+
+        def one(k, c):
             rows_all[g * 4 + k] = norm(raw_all[g * 4 + k], stat_all[g * 2 + k // 2, k % 2])
-            return carry
+            return c
 
         lax.fori_loop(0, QUARTERS, one, 0)
 
-    def first_products(j, steps):
-        g = order[j]
-        for s in steps:
+        def step(s, c):
             products(s, g)
             for o, i in both:
                 quarter_copy(s, j, g, o, i).start()
-
-    stat_step(1)
-    sib_wait(raw_all, zx, 0, 1, -1)
-    first_rows(0)
-    first_products(0, (0,))
-    z_step(raw_all, zx, 2)
-    first_products(0, range(1, EARLY))
-    for s in range(EARLY, STEPS):
-        for o in range(2):
-            w_copy(s, o).start(priority=1)
-    each(pair_copy, 0, "wait")
-    pair_sum[...] = (
-        pair_part[x].astype(F32)
-        + pair_in[0, 0].astype(F32)
-        + pair_in[0, 1].astype(F32)
-        + pair_in[0, 2].astype(F32)
-    ).astype(BF16)
-    each(pair_copy, 1, "start")
-    z_step(raw_all, zx, 3)
-    stat_step(2)
-    sib_wait(raw_all, zx, 2, -2)
-    first_rows(1)
-    first_products(1, range(EARLY))
-    for i in range(2):
-        for copy in turn_copies(i):
-            copy.start(priority=1)
-    for u in range(UNITS):
-        wb_copy(u).start(priority=1)
-    each(pair_copy, 1, "wait")
-    pair_all[x] = (
-        pair_sum[...].astype(F32)
-        + pair_in[1, 0].astype(F32)
-        + pair_in[1, 1].astype(F32)
-        + pair_in[1, 2].astype(F32)
-    ).astype(BF16)
-    each(pair_copy, 2, "start")
-    z_step(raw_all, zx, 4)
-    stat_step(3)
-    sib_wait(raw_all, zx, 3, -3)
-    first_rows(2)
-    first_products(2, range(EARLY))
-    stat_step(4)
-    sib_wait(raw_all, zx, 4)
-    first_rows(3)
-    first_products(3, range(EARLY))
+            pl.when((j == 0) & (s == 0))(lambda: z_step(raw_all, zx, 2))
+            return c
+
+        lax.fori_loop(0, EARLY, step, 0)
+        return carry
+
+    lax.fori_loop(0, QUARTERS, early, 0)
     each(pair_copy, 2, "wait")
     for i in range(2):
         for copy in turn_copies(i):
@@ -450,18 +457,15 @@
         for o, i in both:
             rs_copy(s, o, 0, i).start()
 
-    def added(first, *rest):
-        res = first.astype(F32)
-        for one in rest:
-            res += one.astype(F32)
-        return res
-
     def phase1(s):
         @pl.when(s < EARLY)
         def _():
-            for j in range(QUARTERS):
+            def arrived(j, carry):
                 for o, i in both:
-                    quarter_copy(s, j, order[j], o, i).wait()
+                    quarter_copy(s, j, order(j), o, i).wait()
+                return carry
+
+            lax.fori_loop(0, QUARTERS, arrived, 0)
 
         @pl.when(s >= EARLY)
         def _():
@@ -505,38 +509,35 @@
         vals = kv_all[:, :, HEAD : 2 * HEAD].reshape(TOKENS, HEAD)
         cosine, sine = turn[0, 0] * HEAD**-0.5, turn[0, 1] * HEAD**-0.5
         groups = [v[:, k * 128 : (k + 1) * 128] for v in (left, right) for k in range(3)]
-        query = []
         for h in range(3):
             a, b = groups[2 * h], groups[2 * h + 1]
-            query.append(jnp.concatenate([a * cosine - b * sine, a * sine + b * cosine], 1))
-        scores = lax.dot_general(
-            jnp.concatenate(query, 0).astype(BF16),
-            keys,
-            (((1,), (1,)), ((), ())),
-            preferred_element_type=F32,
-        )
-        probs = []
-        for h in range(3):
-            expos = jnp.where(allowed, jnp.exp(scores[h * ROWS : (h + 1) * ROWS]), 0.0)
-            probs.append((expos / jnp.sum(expos, 1, keepdims=True)).astype(BF16))
-        res = jnp.dot(jnp.concatenate(probs, 0), vals, preferred_element_type=F32).astype(BF16)
-        pieces = [
-            res[h * ROWS : (h + 1) * ROWS, k * 128 : (k + 1) * 128]
-            for h in range(3)
-            for k in range(2)
-        ]
-        return jnp.concatenate(pieces[:3], 1), jnp.concatenate(pieces[3:], 1)
+            heads[h, :, 0:128] = (a * cosine - b * sine).astype(BF16)
+            heads[h, :, 128:256] = (a * sine + b * cosine).astype(BF16)
+
+        def head(h, carry):
+            scores = lax.dot_general(
+                heads[h], keys, (((1,), (1,)), ((), ())), preferred_element_type=F32
+            )
+            expos = jnp.where(allowed, jnp.exp(scores), 0.0)
+            probs = (expos / jnp.sum(expos, 1, keepdims=True)).astype(BF16)
+            heads[h] = jnp.dot(probs, vals, preferred_element_type=F32).astype(BF16)
+            return carry
+
+        lax.fori_loop(0, 3, head, 0)
+        left = jnp.concatenate([heads[0], heads[1, :, 0:128]], 1)
+        right = jnp.concatenate([heads[1, :, 128:256], heads[2]], 1)
+        return left, right
 
     def put(u, block):
         for o in range(2):
             mixed[u // 2, o, 0, 0, u % 2] = block[o * HALF : (o + 1) * HALF]
 
-    def gather_copy(u, n, o, k, i):
+    def gather_copy(u, o, k, i):
         d = dirs[i]
         away, near = (3, 1)[i], (3, 1)[i]
         dev = devs[o][k // 2](d)
         pair = mixed.at[u // 2, o]
-        which = pl.ds(u % 2, 1) if n == 1 else pl.ds(0, 2)
+        which = u % 2
         if k == 0:
             src, dst = pair.at[0, 0, which], pair.at[0, away, which]
         elif k == 1:
@@ -550,13 +551,16 @@
         at = o * 8 + k * 2 + i
         return remote(src, dst, ag_s.at[u, at], ag_r.at[u, at], dev)
 
-    def by_units(u, fn):
-        pl.when((u % 2 == 1) & (u < PAIRED))(lambda: fn(u - 1, 2))
-        pl.when(u >= PAIRED)(lambda: fn(u, 1))
-
-    def gather_first(u, n):
+    def by_units(s, fn):
+        def unit(u, carry):
+            fn(u)
+            return carry
+
+        lax.fori_loop(jnp.where(s == 0, 0, s + 1), s + 2, unit, 0)
+
+    def gather_first(u):
         for o, i in both:
-            gather_copy(u, n, o, 0, i).start()
+            gather_copy(u, o, 0, i).start()
 
     def phase4(s):
         sums = []
@@ -582,47 +586,45 @@
             left, right = attend(*sums)
             put(0, left)
             put(1, right)
-            gather_first(0, 2)
 
         @pl.when(s > 0)
         def _():
             gate, up = sums
             put(s + 1, (gate / (1.0 + jnp.exp(-gate)) * up).astype(BF16))
-            by_units(s + 1, gather_first)
-
-    def phase5(u, n):
+
+        by_units(s, gather_first)
+
+    def phase5(u):
         for o, i in both:
-            gather_copy(u, n, o, 0, i).wait()
-            gather_copy(u, n, o, 1, i).start()
-
-    def phase6(u, n):
+            gather_copy(u, o, 0, i).wait()
+            gather_copy(u, o, 1, i).start()
+
+    def phase6(u):
         for o in range(2):
             for i in range(2):
-                gather_copy(u, n, o, 1, i).wait()
-            for i in range(2):
-                gather_copy(u, n, o, 2, i).start()
-
-    def phase7(u, n):
+                gather_copy(u, o, 1, i).wait()
+            for i in range(2):
+                gather_copy(u, o, 2, i).start()
+
+    def phase7(u):
         for o, i in both:
-            gather_copy(u, n, o, 2, i).wait()
-            gather_copy(u, n, o, 3, i).start()
-
-    def accumulate(u, count):
-        weights = w_back[pl.ds(u, count)].reshape(count * WIDE, FEATS)
-        for o in range(2):
-            for p in range(2):
-                rows = [
-                    mixed[u // 2, o, 2 * p : 2 * p + 2, :, one].reshape(2 * SIDE * HALF, WIDE)
-                    for one in (range(2) if count == 2 else (u % 2,))
-                ]
-                total[o, p * 256 : (p + 1) * 256] += jnp.dot(
-                    jnp.concatenate(rows, 1), weights, preferred_element_type=F32
-                )
-
-    def phase8(u, n):
+            gather_copy(u, o, 2, i).wait()
+            gather_copy(u, o, 3, i).start()
+
+    def accumulate(u):
+        def tile(k, carry):
+            o, p = k // 2, k % 2
+            rows = mixed[u // 2, o, pl.ds(2 * p, 2), :, u % 2].reshape(2 * SIDE * HALF, WIDE)
+            at = pl.ds(pl.multiple_of(p * 256, 256), 256)
+            total[o, at] += jnp.dot(rows, w_back[u], preferred_element_type=F32)
+            return carry
+
+        lax.fori_loop(0, 4, tile, 0)
+
+    def phase8(u):
         for o, i in both:
-            gather_copy(u, n, o, 3, i).wait()
-        accumulate(u, n)
+            gather_copy(u, o, 3, i).wait()
+        accumulate(u)
 
     def slot(t, carry):
         pl.when((t >= EARLY) & (t < STEPS))(lambda: phase0(t))
@@ -646,7 +648,7 @@
 
             @pl.when((s >= 0) & (s < STEPS))
             def _(fn=fn, s=s):
-                by_units(s + 1, fn)
+                by_units(s, fn)
 
         return carry
 
@@ -736,6 +738,7 @@
         pltpu.VMEM((2, 3, ROWS, 128), BF16),
         pltpu.VMEM((ROWS, 128), BF16),
         pltpu.VMEM((4, ROWS, 128), BF16),
+        pltpu.VMEM((3, ROWS, HEAD), BF16),
         pltpu.VMEM((GROUP, ROWS, 512), BF16),
         pltpu.VMEM((STEPS, 2, GROUP, QUARTERS, QUARTER, WIDE), BF16),
         pltpu.VMEM((STEPS, 2, 2, 4, QUARTERS, QUARTER, WIDE), BF16),

time: 140 us -> 140 us (level)
  no operation moved by 1% of the time
where the time goes in v9:
time: 140 us
  Pallas kernels  139 us (99%)
  local copies, waits for them, and re-layouts  1.53 us (1%)
    pallas_call x1, Pallas kernels, per_device(): pl.pallas_call(block_kernel, out_shape=jax.ShapeDtypeStruct((ROWS, FEATS)...  139 us

profile of v9, /device:TPU:32, one launch (start us, length us, event | category | flops | bytes accessed | tf_op | source)
XLA Modules:
  0.0 140.2 jit_solution(1703953847572149394)
XLA Ops:
  0.0 138.6 %shard_map.100 = bf16[64,640]{1,0:T(8,128)(2,1)} custom-call(bf16[64,640]{1,0:T(8,128)(2,1)} %act.1, f32[640]{0:T(1024)} %gain.1, s32[1,1024]{1,0:T(1,128)} %bitcast.1, f32[2,1024,128]{2,1,0:T(8,128)} %constant.2.clone.table, bf16[640,768]{1,0:T(8,128)(2,1)} %w_query.1, bf16[640,512]{1,0:T(8,128)(2,1)} %w_pairs.1, bf16[640,2304]{1,0:T(8,128)(2,1)} %w_gate.1, ...), custom_call_target="tpu_custom_call" | custom-call | tf_op jit(solution)/shard_map/pallas_call | solution.py:775
  138.7 1.5 %copy.12 = bf16[64,640]{1,0:T(8,128)(2,1)} copy(bf16[64,640]{1,0:T(8,128)(2,1)} %shard_map.100) | data formatting | bytes 163840

commit v10 on v9

--- a/solution.py
+++ b/solution.py
@@ -122,7 +122,17 @@
     other = z * 2 + 1 - core
     sibling = (hid, other)
     dirs = (1, -1)
-    devs = ((dev_x, dev_y), (dev_y, dev_x))
+
+    ids_one = {d: jnp.where(core == 0, ids_x[d], ids_y[d]) for d in (1, 3)}
+    ids_two = {d: jnp.where(core == 0, ids_y[d], ids_x[d]) for d in (1, 3)}
+
+    def dev_one(d):
+        return (ids_one[d % SIDE], ffn)
+
+    def dev_two(d):
+        return (ids_two[d % SIDE], ffn)
+
+    devs = ((dev_one, dev_two), (dev_two, dev_one))
 
     barrier = pltpu.get_barrier_semaphore()
     partners = [dev_x(d) for d in (1, 2, 3)] + [dev_y(d) for d in (1, 2, 3)]
@@ -270,9 +280,11 @@
     both = [(o, i) for o in range(2) for i in range(2)]
     rel_x = [mod4(k - x) for k in range(SIDE)]
     rel_y = [mod4(k - y) for k in range(SIDE)]
+    x_y = [rel_x[h // SIDE] * SIDE + rel_y[h % SIDE] for h in range(GROUP)]
+    y_x = [rel_y[h % SIDE] * SIDE + rel_x[h // SIDE] for h in range(GROUP)]
     places = (
-        [rel_x[h // SIDE] * SIDE + rel_y[h % SIDE] for h in range(GROUP)],
-        [rel_y[h % SIDE] * SIDE + rel_x[h // SIDE] for h in range(GROUP)],
+        [jnp.where(core == 0, a, b) for a, b in zip(x_y, y_x)],
+        [jnp.where(core == 0, b, a) for a, b in zip(x_y, y_x)],
     )
 
     def products(s, g):
@@ -660,7 +672,7 @@
         g = block // SIDE
         o = g // 2
         px = mod4(block % SIDE - x)
-        place = jnp.where(o == 0, rel_y[k] * SIDE + px, px * SIDE + rel_y[k])
+        place = jnp.where(o == core, rel_y[k] * SIDE + px, px * SIDE + rel_y[k])
         first = pl.multiple_of(place * HALF + (g % 2) * QUARTER, QUARTER)
         return total[o, pl.ds(first, QUARTER)]
 
@@ -779,7 +791,7 @@
         out_specs=vmem,
         scratch_shapes=scratch,
         compiler_params=pltpu.CompilerParams(
-            collective_id=0, has_side_effects=True, vmem_limit_bytes=60 * 1024 * 1024
+            collective_id=0, has_side_effects=True, vmem_limit_bytes=54784 * 1024
         ),
     )(
         activations,

time: 140 us -> 140 us (level)
  Pallas kernels: 139 us -> 137 us
    pallas_call x1, Pallas kernels: 139 us -> 137 us  [per_device(): pl.pallas_call(block_kernel, out_shape=jax.ShapeDtypeStruct((ROWS, FEATS)...]
    unnamed x1 -> x7, local copies, waits for them, and re-layouts: 1.53 us -> 2.9 us
where the time goes in v10:
time: 140 us
  Pallas kernels  137 us (98%)
  local copies, waits for them, and re-layouts  2.9 us (2%)
    pallas_call x1, Pallas kernels, per_device(): pl.pallas_call(block_kernel, out_shape=jax.ShapeDtypeStruct((ROWS, FEATS)...  137 us
    unnamed x7, local copies, waits for them, and re-layouts  2.9 us

profile of v10, /device:TPU:32, one launch (start us, length us, event | category | flops | bytes accessed | tf_op | source)
XLA Modules:
  0.0 140.1 jit_solution(10616226299752252291)
XLA Ops:
  0.0 0.0 copy-start
  0.0 0.9 copy-done
  0.9 0.0 copy-start.1
  0.9 0.7 copy-done.1
  1.6 0.0 copy-start.2
  1.6 0.7 copy-done.2
  2.3 137.2 %shard_map.100 = bf16[64,640]{1,0:T(8,128)(2,1)S(1)} custom-call(bf16[64,640]{1,0:T(8,128)(2,1)S(1)} %copy-done, f32[640]{0:T(1024)S(1)} %copy-done.1, s32[1,1024]{1,0:T(1,128)S(1)} %bitcast.1, f32[2,1024,128]{2,1,0:T(8,128)} %constant.2.clone.table, bf16[640,768]{1,0:T(8,128)(2,1)} %w_query.1, bf16[640,512]{1,0:T(8,128)(2,1)} %w_pairs.1, ...), custom_call_target="tpu_custom_call" | custom-call | tf_op jit(solution)/shard_map/pallas_call | solution.py:787
  139.5 0.6 copy.12
Async XLA Ops:
  0.0 0.9 copy-start
  0.9 0.7 copy-start.1
  1.6 0.7 copy-start.2

commit v11 on v10

--- a/solution.py
+++ b/solution.py
@@ -36,9 +36,9 @@
 
 
 def block_kernel(
-    act,
-    gain,
-    seg,
+    act_far,
+    gain_far,
+    seg_far,
     table,
     w_query,
     w_pairs,
@@ -47,6 +47,9 @@
     w_out,
     w_down,
     out,
+    act,
+    gain,
+    seg,
     w_in,
     w_back,
     w_kv,
@@ -95,6 +98,12 @@
     zr_s,
     zr_r,
 ):
+    own_copies = [
+        pltpu.make_async_copy(far, near, m_sem.at[11 + k])
+        for k, (far, near) in enumerate(((act_far, act), (gain_far, gain), (seg_far, seg)))
+    ]
+    for copy in own_copies:
+        copy.start(priority=1)
     hid = lax.axis_index("hid")
     ffn = lax.axis_index("ffn")
     x, y = hid // SIDE, hid % SIDE
@@ -190,6 +199,8 @@
     for s in range(EARLY):
         for o in range(2):
             w_copy(s, o).start(priority=1)
+    for copy in own_copies:
+        copy.wait()
     pl.semaphore_wait(barrier, len(partners))
 
     def stat_copy(a, d):
@@ -733,9 +744,12 @@
 
 def per_device(activations, ln_gain, segments, w_query, w_key_value, w_gate, w_up, w_out, w_down):
     vmem = pl.BlockSpec(memory_space=pltpu.VMEM)
-    anywhere = pl.BlockSpec(memory_space=pl.ANY)
+    far = pl.BlockSpec(memory_space=pltpu.HBM)
     dma = pltpu.SemaphoreType.DMA
     scratch = [
+        pltpu.VMEM((ROWS, FEATS), BF16),
+        pltpu.VMEM((FEATS,), F32),
+        pltpu.VMEM((1, TOKENS), jnp.int32),
         pltpu.VMEM((STEPS, FEATS, 2 * WIDE), BF16),
         pltpu.VMEM((UNITS, WIDE, FEATS), BF16),
         pltpu.VMEM((FEATS, 512), BF16),
@@ -766,7 +780,7 @@
         pltpu.VMEM((4, 2, 4, QUARTER, FEATS), BF16),
         dma((STEPS, 2)),
         dma((UNITS,)),
-        dma((11,)),
+        dma((14,)),
         dma((7, 3)),
         dma((7, 3)),
         dma((8, 2)),
@@ -787,16 +801,16 @@
     return pl.pallas_call(
         block_kernel,
         out_shape=jax.ShapeDtypeStruct((ROWS, FEATS), BF16),
-        in_specs=[vmem, vmem, vmem] + [anywhere] * 7,
+        in_specs=[far] * 10,
         out_specs=vmem,
         scratch_shapes=scratch,
         compiler_params=pltpu.CompilerParams(
             collective_id=0, has_side_effects=True, vmem_limit_bytes=54784 * 1024
         ),
     )(
-        activations,
-        ln_gain,
-        segments.reshape(1, TOKENS),
+        pltpu.with_memory_space_constraint(activations, pltpu.HBM),
+        pltpu.with_memory_space_constraint(ln_gain, pltpu.HBM),
+        pltpu.with_memory_space_constraint(segments.reshape(1, TOKENS), pltpu.HBM),
         jnp.asarray(tables()),
         w_query,
         w_key_value,

time: 140 us -> 138 us (0.986)
  local copies, waits for them, and re-layouts: 2.9 us -> 0.64 us
    unnamed x7 -> x1, local copies, waits for them, and re-layouts: 2.9 us -> 0.64 us
where the time goes in v11:
time: 138 us
  Pallas kernels  137 us (99%)
    pallas_call x1, Pallas kernels, per_device(): pl.pallas_call(block_kernel, out_shape=jax.ShapeDtypeStruct((ROWS, FEATS)...  137 us

profile of v11, /device:TPU:32, one launch (start us, length us, event | category | flops | bytes accessed | tf_op | source)
XLA Modules:
  0.0 137.9 jit_solution(2533383787126354322)
XLA Ops:
  0.0 137.2 %shard_map.100 = bf16[64,640]{1,0:T(8,128)(2,1)S(1)} custom-call(bf16[64,640]{1,0:T(8,128)(2,1)} %act_far.1, f32[640]{0:T(1024)} %gain_far.1, s32[1,1024]{1,0:T(1,128)} %bitcast.1, f32[2,1024,128]{2,1,0:T(8,128)} %constant.2.clone.table, bf16[640,768]{1,0:T(8,128)(2,1)} %w_query.1, bf16[640,512]{1,0:T(8,128)(2,1)} %w_pairs.1, bf16[640,2304]{1,0:T(8,128)(2,1)} %w_gate.1, ...), custom_call_target="tpu_custom_call" | custom-call | tf_op jit(solution)/shard_map/pallas_call | solution.py:801
  137.3 0.6 copy.12

commit v12 on v11

--- a/solution.py
+++ b/solution.py
@@ -278,13 +278,13 @@
             res += one.astype(F32)
         return res
 
-    def quarter_copy(s, j, g, o, i):
+    def quarter_copy(s, g, o, i):
         at = o * 2 + i
         return remote(
             part.at[s, o, pl.ds((6, 10)[i], 4), g],
             land1.at[s, o, i, :, g],
-            rq_s.at[s * QUARTERS + j, at],
-            rq_r.at[s * QUARTERS + j, at],
+            rq_s.at[s * QUARTERS + g, at],
+            rq_r.at[s * QUARTERS + g, at],
             devs[o][0](dirs[i]),
         )
 
@@ -426,7 +426,7 @@
         def step(s, c):
             products(s, g)
             for o, i in both:
-                quarter_copy(s, j, g, o, i).start()
+                quarter_copy(s, g, o, i).start()
             pl.when((j == 0) & (s == 0))(lambda: z_step(raw_all, zx, 2))
             return c
 
@@ -451,14 +451,10 @@
     for u in range(UNITS):
         wb_copy(u).wait()
 
-    far1 = ((6, 4), (10, 4))
-    near1 = ((4, 2), (14, 2))
-
     def rs_copy(s, o, k, i):
         at = o * 8 + k * 2 + i
-        if k < 2:
-            first, size = (far1, near1)[k][i]
-            src = part.at[s, o, pl.ds(first, size)]
+        if k == 1:
+            src = part.at[s, o, pl.ds((4, 14)[i], 2)]
         elif k == 2:
             src = near_sum.at[s, o, pl.ds((6, 10)[i], 4)]
         else:
@@ -474,30 +470,22 @@
     def phase0(s):
         def tile(g, carry):
             products(s, g)
+            for o, i in both:
+                quarter_copy(s, g, o, i).start()
             return carry
 
         lax.fori_loop(0, QUARTERS, tile, 0)
+
+    def phase1(s):
+        def arrived(g, carry):
+            for o, i in both:
+                quarter_copy(s, g, o, i).wait()
+            return carry
+
+        lax.fori_loop(0, QUARTERS, arrived, 0)
         for o, i in both:
-            rs_copy(s, o, 0, i).start()
-
-    def phase1(s):
-        @pl.when(s < EARLY)
-        def _():
-            def arrived(j, carry):
-                for o, i in both:
-                    quarter_copy(s, j, order(j), o, i).wait()
-                return carry
-
-            lax.fori_loop(0, QUARTERS, arrived, 0)
-
-        @pl.when(s >= EARLY)
-        def _():
-            for o, i in both:
-                rs_copy(s, o, 0, i).wait()
-
-        for o, i in both:
-            first, size = near1[i]
-            part[s, o, first : first + size] += land1[s, o, i, 2 - 2 * i : 4 - 2 * i]
+            first = (4, 14)[i]
+            part[s, o, first : first + 2] += land1[s, o, i, 2 - 2 * i : 4 - 2 * i]
             rs_copy(s, o, 1, i).start()
 
     def phase2(s):
@@ -787,8 +775,8 @@
         dma((8, 2)),
         dma((5, 2)),
         dma((5, 2)),
-        dma((EARLY * QUARTERS, 4)),
-        dma((EARLY * QUARTERS, 4)),
+        dma((STEPS * QUARTERS, 4)),
+        dma((STEPS * QUARTERS, 4)),
         dma((8, 2)),
         dma((8, 2)),
         dma((STEPS, 16)),

time: 138 us -> 138 us (level)
  no operation moved by 1% of the time
where the time goes in v12:
time: 138 us
  Pallas kernels  138 us (100%)
    pallas_call x1, Pallas kernels, per_device(): pl.pallas_call(block_kernel, out_shape=jax.ShapeDtypeStruct((ROWS, FEATS)...  138 us

profile of v12, /device:TPU:32, one launch (start us, length us, event | category | flops | bytes accessed | tf_op | source)
XLA Modules:
  0.0 138.2 jit_solution(1512845895459069854)
XLA Ops:
  0.0 137.6 %shard_map.100 = bf16[64,640]{1,0:T(8,128)(2,1)S(1)} custom-call(bf16[64,640]{1,0:T(8,128)(2,1)} %act_far.1, f32[640]{0:T(1024)} %gain_far.1, s32[1,1024]{1,0:T(1,128)} %bitcast.1, f32[2,1024,128]{2,1,0:T(8,128)} %constant.2.clone.table, bf16[640,768]{1,0:T(8,128)(2,1)} %w_query.1, bf16[640,512]{1,0:T(8,128)(2,1)} %w_pairs.1, bf16[640,2304]{1,0:T(8,128)(2,1)} %w_gate.1, ...), custom_call_target="tpu_custom_call" | custom-call | tf_op jit(solution)/shard_map/pallas_call | solution.py:789
  137.6 0.6 copy.12

commit v13 on v11

--- a/solution.py
+++ b/solution.py
@@ -651,7 +651,7 @@
 
     def slot(t, carry):
         pl.when((t >= EARLY) & (t < STEPS))(lambda: phase0(t))
-        for k, fn in ((2, phase1), (4, phase2), (5, phase3)):
+        for k, fn in ((2, phase1), (3, phase2), (4, phase3)):
             s = t - k
             pl.when((s >= 0) & (s < STEPS))(lambda fn=fn, s=s: fn(s))
 
@@ -663,10 +663,10 @@
                 if j == 4:
                     sib_wait(kv_all, zk, 0, 1, -1, 2, -2, 3, -3, 4)
 
-        s4 = t - 6
+        s4 = t - 5
         pl.when((s4 >= 0) & (s4 < STEPS))(lambda: phase4(s4))
 
-        for k, fn in ((7, phase5), (8, phase6), (9, phase7), (10, phase8)):
+        for k, fn in ((6, phase5), (7, phase6), (8, phase7), (9, phase8)):
             s = t - k
 
             @pl.when((s >= 0) & (s < STEPS))
@@ -675,7 +675,7 @@
 
         return carry
 
-    lax.fori_loop(2, STEPS + 10, slot, 0)
+    lax.fori_loop(2, STEPS + 9, slot, 0)
 
     offsets = (4, 3, -3, 2, -2, 1, -1, 0)
 

time: 138 us -> 139 us (level)
  no operation moved by 1% of the time
where the time goes in v13:
time: 139 us
  Pallas kernels  138 us (99%)
    pallas_call x1, Pallas kernels, per_device(): pl.pallas_call(block_kernel, out_shape=jax.ShapeDtypeStruct((ROWS, FEATS)...  138 us

profile of v13, /device:TPU:32, one launch (start us, length us, event | category | flops | bytes accessed | tf_op | source)
XLA Modules:
  0.0 138.6 jit_solution(12343438505009701860)
XLA Ops:
  0.0 138.0 %shard_map.100 = bf16[64,640]{1,0:T(8,128)(2,1)S(1)} custom-call(bf16[64,640]{1,0:T(8,128)(2,1)} %act_far.1, f32[640]{0:T(1024)} %gain_far.1, s32[1,1024]{1,0:T(1,128)} %bitcast.1, f32[2,1024,128]{2,1,0:T(8,128)} %constant.2.clone.table, bf16[640,768]{1,0:T(8,128)(2,1)} %w_query.1, bf16[640,512]{1,0:T(8,128)(2,1)} %w_pairs.1, bf16[640,2304]{1,0:T(8,128)(2,1)} %w_gate.1, ...), custom_call_target="tpu_custom_call" | custom-call | tf_op jit(solution)/shard_map/pallas_call | solution.py:801
  138.0 0.6 copy.12
